TPU v7x, 32 devices: a whole 2x2x4 slice. The times are simulated.
32 devices in a mesh: dp: 8 (over z, x), seq: 4 (over y, core).
Axes of the slice: x: 2, y: 2, z: 4, core: 2. Of those that a mesh axis runs over, the one named last changes fastest.
Arguments:
- tokens: bfloat16 [16, 1024, 1024], P('dp', 'seq'), may hold values from -6 to 6
- enc_states: bfloat16 [16, 1024, 1024], P('dp', 'seq'), may hold values from -6 to 6
- dec_lengths: int32 [16], P('dp'), may hold values from 129 to 1024, as said below
- enc_lengths: int32 [16], P('dp'), may hold values from 256 to 1024, as said below
- adapter_step: int32 [16], P('dp'), may hold values from 0 to 4
- out_grad: bfloat16 [16, 1024, 1024], P('dp', 'seq'), may hold values from -6 to 6
- self_query: bfloat16 [1024, 1024], replicated, may hold values from -0.1875 to 0.1875
- self_key: bfloat16 [1024, 1024], replicated, may hold values from -0.1875 to 0.1875
- self_value: bfloat16 [1024, 1024], replicated, may hold values from -0.1875 to 0.1875
- self_out: bfloat16 [1024, 1024], replicated, may hold values from -0.75 to 0.75
- cross_query: bfloat16 [1024, 1024], replicated, may hold values from -0.1875 to 0.1875
- cross_key: bfloat16 [1024, 1024], replicated, may hold values from -0.1875 to 0.1875
- cross_value: bfloat16 [1024, 1024], replicated, may hold values from -0.1875 to 0.1875
- cross_out: bfloat16 [1024, 1024], replicated, may hold values from -0.75 to 0.75
- ffn_in: bfloat16 [1024, 4096], replicated, may hold values from -0.1875 to 0.1875
- ffn_out: bfloat16 [4096, 1024], replicated, may hold values from -0.09375 to 0.09375
- adapter_down: bfloat16 [1024, 512], replicated, may hold values from -0.1875 to 0.1875
- adapter_up: bfloat16 [512, 1024], replicated, may hold values from -0.25 to 0.25
- ln_gain: float32 [3, 1024], replicated, may hold values from 0.5 to 1.5
- ln_bias: float32 [3, 1024], replicated, may hold values from -1.2 to 1.2
Outputs:
- layer_output: bfloat16 [16, 1024, 1024], P('dp', 'seq')
- token_grad: bfloat16 [16, 1024, 1024], P('dp', 'seq')
- enc_grad: bfloat16 [16, 1024, 1024], P('dp', 'seq')
- adapter_down_grad: float32 [1024, 512], replicated
- adapter_up_grad: float32 [512, 1024], replicated
- ln_gain_grad: float32 [3, 1024], replicated
- ln_bias_grad: float32 [3, 1024], replicated
Inputs may be any that keep to these rules, and one draw needn't show every extreme that they name: `dec_lengths`: lengths come from buckets of 256, 512 and 1024 positions, each more than half its bucket; among the 2 sequences of each index of dp, one has length 1024. `enc_lengths`: among the 2 sequences of each index of dp, one has length 1024.
All inputs are finite; a program needn't handle non-finite values.
Results may differ from a plain program's by a relative error of at most 0.02.
Values may be sent and summed in bfloat16 or wider, within the bound.
No kernel may reach another device: no remote copies, remote signals or barrier semaphores. Data moves between devices by JAX's collectives and lax.ppermute only.
A program may use at most 320 MiB of HBM per device.

v0:
```python
from functools import partial

import jax
import jax.numpy as jnp
from jax import lax
from jax.sharding import PartitionSpec as P

HEADS = 16
HEAD_DIM = 64


EPS = 1e-05
NEGATIVE = -1e30


def layer_norm(summed, gain_row, shift_row):
    center = summed - jnp.mean(summed, axis=-1, keepdims=True)
    spread = jnp.mean(center * center, axis=-1, keepdims=True)
    return center * lax.rsqrt(spread + EPS) * gain_row + shift_row


def project(activation, weight):
    return jnp.einsum("std,de->ste", activation, weight, preferred_element_type=jnp.float32)


def project_back(gradient, weight):
    return jnp.einsum("ste,de->std", gradient, weight, preferred_element_type=jnp.float32)


def weight_grad(activation, gradient):
    return jnp.einsum("std,ste->de", activation, gradient, preferred_element_type=jnp.float32)


def split_heads(value):
    return value.reshape(value.shape[0], value.shape[1], HEADS, HEAD_DIM)


def score_table(queries, all_keys, allowed):
    scores = jnp.einsum(
        "sqhd,skhd->shqk",
        split_heads(queries),
        split_heads(all_keys),
        preferred_element_type=jnp.float32,
    ) * HEAD_DIM ** (-0.5)
    return jnp.where(allowed[:, None], scores, NEGATIVE)


def attend(queries, all_keys, values, allowed):
    scores = score_table(queries, all_keys, allowed)
    highest = jnp.max(scores, axis=-1, keepdims=True)
    weights = jnp.exp(scores - highest)
    summed = jnp.sum(weights, axis=-1, keepdims=True)
    probabilities = weights / summed
    attended = jnp.einsum(
        "shqk,skhd->sqhd",
        probabilities.astype(jnp.bfloat16),
        split_heads(values),
        preferred_element_type=jnp.float32,
    )
    return (attended.reshape(queries.shape).astype(jnp.bfloat16), highest, summed)


def attend_back(queries, all_keys, values, allowed, highest, summed, grad_attended):
    scale_factor = HEAD_DIM ** (-0.5)
    scores = score_table(queries, all_keys, allowed)
    probabilities = jnp.exp(scores - highest) / summed
    grad_heads = split_heads(grad_attended)
    grad_probs = jnp.einsum(
        "sqhd,skhd->shqk", grad_heads, split_heads(values), preferred_element_type=jnp.float32
    )
    grad_values = jnp.einsum(
        "shqk,sqhd->skhd",
        probabilities.astype(jnp.bfloat16),
        grad_heads,
        preferred_element_type=jnp.float32,
    )
    grad_scores = probabilities * (
        grad_probs - jnp.sum(probabilities * grad_probs, axis=-1, keepdims=True)
    )
    grad_low = grad_scores.astype(jnp.bfloat16)
    grad_queries = (
        jnp.einsum(
            "shqk,skhd->sqhd", grad_low, split_heads(all_keys), preferred_element_type=jnp.float32
        )
        * scale_factor
    )
    grad_keys = (
        jnp.einsum(
            "shqk,sqhd->skhd", grad_low, split_heads(queries), preferred_element_type=jnp.float32
        )
        * scale_factor
    )
    return (
        grad_queries.reshape(queries.shape),
        grad_keys.reshape(all_keys.shape),
        grad_values.reshape(all_keys.shape),
    )


def per_device(
    tokens,
    enc_states,
    dec_lengths,
    enc_lengths,
    adapter_step,
    out_grad,
    self_query,
    self_key,
    self_value,
    self_out,
    cross_query,
    cross_key,
    cross_value,
    cross_out,
    ffn_in,
    ffn_out,
    adapter_down,
    adapter_up,
    ln_gain,
    ln_bias,
):
    group_size = lax.axis_size("seq")
    member = lax.axis_index("seq")
    local_len = tokens.shape[1]
    full_len = local_len * group_size
    enc_full = enc_states.shape[1] * group_size
    query_pos = member * local_len + jnp.arange(local_len)
    key_pos = jnp.arange(full_len)
    causal = (key_pos[None, None, :] <= query_pos[None, :, None]) & (
        key_pos[None, None, :] < dec_lengths[:, None, None]
    )
    enc_reach = jnp.arange(enc_full)[None, None, :] < enc_lengths[:, None, None]
    factor = ((1.0 + adapter_step.astype(jnp.float32)) * 0.25)[:, None, None]
    queries = project(tokens, self_query).astype(jnp.bfloat16)
    own_keys = project(tokens, self_key).astype(jnp.bfloat16)
    own_values = project(tokens, self_value).astype(jnp.bfloat16)
    all_keys, all_values = (
        lax.all_gather(own_keys, "seq", axis=1, tiled=True),
        lax.all_gather(own_values, "seq", axis=1, tiled=True),
    )
    attended, self_high, self_summed = attend(queries, all_keys, all_values, causal)
    first_total = tokens.astype(jnp.float32) + project(attended, self_out)
    first_norm, first_pull = jax.vjp(layer_norm, first_total, ln_gain[0], ln_bias[0])
    cross_queries = project(first_norm.astype(jnp.bfloat16), cross_query).astype(jnp.bfloat16)
    own_cross_keys = project(enc_states, cross_key).astype(jnp.bfloat16)
    own_cross_values = project(enc_states, cross_value).astype(jnp.bfloat16)
    cross_keys, cross_values = (
        lax.all_gather(own_cross_keys, "seq", axis=1, tiled=True),
        lax.all_gather(own_cross_values, "seq", axis=1, tiled=True),
    )
    cross_attended, cross_high, cross_summed = attend(
        cross_queries, cross_keys, cross_values, enc_reach
    )
    second_total = first_norm + project(cross_attended, cross_out)
    second_norm, second_pull = jax.vjp(layer_norm, second_total, ln_gain[1], ln_bias[1])
    second_low = second_norm.astype(jnp.bfloat16)
    inner_act = project(second_low, ffn_in)
    hidden = jax.nn.gelu(inner_act, approximate=False).astype(jnp.bfloat16)
    adapter_in = project(second_low, adapter_down)
    adapter_hidden = (factor * jax.nn.silu(adapter_in)).astype(jnp.bfloat16)
    update = project(hidden, ffn_out) + project(adapter_hidden, adapter_up)
    layer_output, third_pull = jax.vjp(layer_norm, second_norm + update, ln_gain[2], ln_bias[2])
    grad_third, gain_three, shift_three = third_pull(out_grad.astype(jnp.float32))
    grad_update = grad_third.astype(jnp.bfloat16)
    adapter_up_grad = weight_grad(adapter_hidden, grad_update)
    silu_pull = jax.vjp(jax.nn.silu, adapter_in)[1]
    grad_adapter_in = silu_pull(factor * project_back(grad_update, adapter_up))[0].astype(
        jnp.bfloat16
    )
    adapter_down_grad = weight_grad(second_low, grad_adapter_in)
    adapter_down_grad, adapter_up_grad = lax.psum(
        (adapter_down_grad, adapter_up_grad), ("dp", "seq")
    )
    gelu_pull = jax.vjp(partial(jax.nn.gelu, approximate=False), inner_act)[1]
    grad_inner = gelu_pull(project_back(grad_update, ffn_out))[0].astype(jnp.bfloat16)
    grad_second = (
        grad_third + project_back(grad_inner, ffn_in) + project_back(grad_adapter_in, adapter_down)
    )
    grad_second_in, gain_two, shift_two = second_pull(grad_second)
    grad_cross_attended = project_back(grad_second_in.astype(jnp.bfloat16), cross_out).astype(
        jnp.bfloat16
    )
    grad_cross_queries, grad_cross_keys, grad_cross_values = attend_back(
        cross_queries,
        cross_keys,
        cross_values,
        enc_reach,
        cross_high,
        cross_summed,
        grad_cross_attended,
    )
    owned_cross_keys, owned_cross_values = (
        lax.psum_scatter(
            grad_cross_keys.astype(jnp.bfloat16), "seq", scatter_dimension=1, tiled=True
        ).astype(jnp.float32),
        lax.psum_scatter(
            grad_cross_values.astype(jnp.bfloat16), "seq", scatter_dimension=1, tiled=True
        ).astype(jnp.float32),
    )
    enc_grad = project_back(owned_cross_keys.astype(jnp.bfloat16), cross_key) + project_back(
        owned_cross_values.astype(jnp.bfloat16), cross_value
    )
    grad_first = grad_second_in + project_back(grad_cross_queries.astype(jnp.bfloat16), cross_query)
    grad_first_in, gain_one, shift_one = first_pull(grad_first)
    grad_attended = project_back(grad_first_in.astype(jnp.bfloat16), self_out).astype(jnp.bfloat16)
    grad_queries, grad_keys, grad_values = attend_back(
        queries, all_keys, all_values, causal, self_high, self_summed, grad_attended
    )
    owned_keys, owned_values = (
        lax.psum_scatter(
            grad_keys.astype(jnp.bfloat16), "seq", scatter_dimension=1, tiled=True
        ).astype(jnp.float32),
        lax.psum_scatter(
            grad_values.astype(jnp.bfloat16), "seq", scatter_dimension=1, tiled=True
        ).astype(jnp.float32),
    )
    token_grad = grad_first_in + project_back(grad_queries.astype(jnp.bfloat16), self_query)
    token_grad = (
        token_grad
        + project_back(owned_keys.astype(jnp.bfloat16), self_key)
        + project_back(owned_values.astype(jnp.bfloat16), self_value)
    )
    gain_grads = jnp.stack([gain_one, gain_two, gain_three])
    shift_grads = jnp.stack([shift_one, shift_two, shift_three])
    gain_grads, shift_grads = lax.psum((gain_grads, shift_grads), ("dp", "seq"))
    return (
        layer_output.astype(jnp.bfloat16),
        token_grad.astype(jnp.bfloat16),
        enc_grad.astype(jnp.bfloat16),
        adapter_down_grad,
        adapter_up_grad,
        gain_grads,
        shift_grads,
    )


def solution(mesh):
    return jax.shard_map(
        per_device,
        mesh=mesh,
        in_specs=(
            P("dp", "seq", None),
            P("dp", "seq", None),
            P("dp"),
            P("dp"),
            P("dp"),
            P("dp", "seq", None),
            P(),
            P(),
            P(),
            P(),
            P(),
            P(),
            P(),
            P(),
            P(),
            P(),
            P(),
            P(),
            P(),
            P(),
        ),
        out_specs=(
            P("dp", "seq", None),
            P("dp", "seq", None),
            P("dp", "seq", None),
            P(),
            P(),
            P(),
            P(),
        ),
        check_vma=False,
    )
```

profile of v0, /device:TPU:0, one launch (start us, length us, event | category | flops | bytes accessed | tf_op | source)
XLA Modules:
  0.0 730.9 jit_solution(16712230045557489671)
XLA Ops:
  7.2 4.3 fusion.108
  11.6 3.8 fusion.102
  15.5 4.1 fusion.120
  19.8 4.4 fusion.114
  24.3 3.8 fusion.105
  28.2 1.9 copy.54
  33.3 15.6 %all-gather.7.cloned.1.call-done = bf16[2,1024,1024]{2,1,0:T(8,128)(2,1)} async-done(((bf16[2,256,1024]{2,1,0:T(8,128)(2,1)}), bf16[2,1024,1024]{2,1,0:T(8,128)(2,1)}) %all-gather.7.cloned.1.call-update) | async-done | bytes 4194320 | tf_op jit(solution)/shard_map/all_gather | solution.py:138
  48.9 6.2 copy.55
  55.1 19.1 %fusion.156 = (f32[2,16,256]{2,1,0:T(8,128)S(1)}, f32[2,16,256,1024]{3,2,1,0:T(8,128)}) fusion(pred[2,256,1024]{2,1,0:T(8,128)(4,1)} %broadcast_and_fusion, bf16[2,256,16,64]{1,3,2,0:T(8,128)(2,1)S(1)} %bitcast.202, bf16[2,1024,16,64]{1,3,2,0:T(8,128)(2,1)} %bitcast.198), kind=kOutput, calls=%fused_computation.195 | convolution fusion | flops 1107297280 | bytes 39354368 | tf_op jit(solution)/shard_map/sub | solution.py:51
  74.2 11.4 %all-gather.5.cloned.1.call-done = bf16[2,1024,1024]{2,1,0:T(8,128)(2,1)} async-done(((bf16[2,256,1024]{2,1,0:T(8,128)(2,1)}), bf16[2,1024,1024]{2,1,0:T(8,128)(2,1)}) %all-gather.5.cloned.1.call-update) | async-done | bytes 4194320 | tf_op jit(solution)/shard_map/all_gather | solution.py:139
  85.6 6.2 copy.53
  91.8 17.5 %fusion.96 = bf16[2,16,64,256]{3,2,1,0:T(8,128)(2,1)} fusion(bf16[2,1024,16,64]{1,3,2,0:T(8,128)(2,1)} %bitcast.206, f32[2,16,256,1024]{3,2,1,0:T(8,128)} %get-tuple-element.39, f32[2,16,256]{2,1,0:T(8,128)S(1)} %get-tuple-element.38), kind=kOutput, calls=%fused_computation.135 | convolution fusion | flops 1091043328 | bytes 38830080 | tf_op jit(solution)/shard_map/shqk,skhd->sqhd/dot_general | solution.py:54
  109.3 3.3 fusion.157
  113.9 2.3 fusion.117
  116.2 1.6 copy.58
  117.9 4.4 all-gather.11.cloned.1.call-done
  122.2 6.2 copy.59
  128.4 18.2 %fusion.158 = (f32[2,16,256]{2,1,0:T(8,128)S(1)}, f32[2,16,256,1024]{3,2,1,0:T(8,128)}) fusion(pred[2,1024]{1,0:T(4,128)(4,1)S(1)} %iota_compare_fusion.1, bf16[2,256,16,64]{1,3,2,0:T(8,128)(2,1)S(1)} %bitcast.204, bf16[2,1024,16,64]{1,3,2,0:T(8,128)(2,1)} %bitcast.200), kind=kOutput, calls=%fused_computation.197 | convolution fusion | flops 1107297280 | bytes 38832128 | tf_op jit(solution)/shard_map/sub | solution.py:51
  146.7 12.1 %all-gather.9.cloned.1.call-done = bf16[2,1024,1024]{2,1,0:T(8,128)(2,1)} async-done(((bf16[2,256,1024]{2,1,0:T(8,128)(2,1)}), bf16[2,1024,1024]{2,1,0:T(8,128)(2,1)}) %all-gather.9.cloned.1.call-update) | async-done | bytes 4194320 | tf_op jit(solution)/shard_map/all_gather | solution.py:149
  158.7 6.2 copy.57
  164.9 15.0 %fusion.99 = bf16[2,16,64,256]{3,2,1,0:T(8,128)(2,1)S(1)} fusion(bf16[2,1024,16,64]{1,3,2,0:T(8,128)(2,1)} %bitcast.208, f32[2,16,256,1024]{3,2,1,0:T(8,128)} %get-tuple-element.43, f32[2,16,256]{2,1,0:T(8,128)S(1)} %get-tuple-element.42), kind=kOutput, calls=%fused_computation.136 | convolution fusion | flops 1091043328 | bytes 38830080 | tf_op jit(solution)/shard_map/shqk,skhd->sqhd/dot_general | solution.py:54
  179.9 3.7 fusion.159
  184.4 11.2 %fusion.82 = (u8[256,4096]{1,0:T(8,128)(4,1)S(1)}, u8[256,4096]{1,0:T(8,128)(4,1)}, f32[2,256,4096]{2,1,0:T(8,128)S(1)}) fusion(bf16[2,256,1024]{2,1,0:T(8,128)(2,1)S(1)} %fusion.85, bf16[1024,4096]{1,0:T(8,128)(2,1)} %param.34), kind=kOutput, calls=%fused_computation.124 | convolution fusion | flops 4320133120 | bytes 19922944 | tf_op jit(solution)/shard_map/std,de->ste/dot_general | solution.py:23
  195.6 1.7 fusion.133
  197.6 18.3 %fusion.10 = f32[2,256,4096]{2,1,0:T(8,128)S(1)} fusion(f32[2,256,4096]{2,1,0:T(8,128)S(1)} %get-tuple-element.46, u8[256,4096]{1,0:T(8,128)(4,1)S(1)} %copy-done.18, u8[256,4096]{1,0:T(8,128)(4,1)S(1)} %get-tuple-element.7), kind=kLoop, calls=%fused_computation.21 | loop fusion | flops 140509184 | bytes 18874368 | tf_op jit(solution)/shard_map/erfc | solution.py:158
  215.9 11.9 %fusion.13 = f32[2,256,1024]{2,1,0:T(8,128)} fusion(bf16[4096,1024]{1,0:T(8,128)(2,1)} %param.35, f32[2,256,4096]{2,1,0:T(8,128)S(1)} %fusion.10, f32[2,256,4096]{2,1,0:T(8,128)S(1)} %get-tuple-element.46), kind=kOutput, calls=%fused_computation.29 | convolution fusion | flops 4301258752 | bytes 27262976 | tf_op jit(solution)/shard_map/std,de->ste/dot_general | solution.py:23
  227.8 3.1 fusion.160
  230.9 1.4 fusion.47
  232.3 1.7 fusion.48
  234.0 1.8 add_convert_fusion.6
  235.8 14.8 %add_convert_fusion = bf16[2,256,4096]{2,1,0:T(8,128)(2,1)} fusion(f32[2,256,4096]{2,1,0:T(8,128)} %copy-done.5, f32[2,256,4096]{2,1,0:T(8,128)} %copy-done.4, bf16[2,256,1024]{2,1,0:T(8,128)(2,1)S(1)} %get-tuple-element.28, bf16[4096,1024]{1,0:T(8,128)(2,1)} %param.35), kind=kOutput, calls=%fused_computation.37 | convolution fusion | flops 4324327424 | bytes 30408704 | tf_op jit(solution)/shard_map/ste,de->std/dot_general | solution.py:27
  252.9 7.3 %fusion.15 = f32[2,256,1024]{2,1,0:T(8,128)S(1)} fusion(bf16[2,256,4096]{2,1,0:T(8,128)(2,1)S(1)} %copy-done.60, bf16[1024,4096]{1,0:T(8,128)(2,1)} %param.34), kind=kOutput, calls=%fused_computation.31 | convolution fusion | flops 4294967296 | bytes 14680064 | tf_op jit(solution)/shard_map/ste,de->std/dot_general | solution.py:27
  260.2 2.3 multiply_reduce_fusion.2
  264.6 2.3 fusion.123
  266.9 1.5 copy.61
  268.4 23.4 %multiply_reduce_fusion.1 = (f32[2,16,256]{2,1,0:T(8,128)S(1)}, f32[2,16,256,1024]{3,2,1,0:T(8,128)}) fusion(f32[2,16,256,1024]{3,2,1,0:T(8,128)} %get-tuple-element.43, f32[2,16,256]{2,1,0:T(8,128)S(1)} %get-tuple-element.42, bf16[2,256,16,64]{1,3,2,0:T(8,128)(2,1)S(1)} %bitcast.212, bf16[2,1024,16,64]{1,3,2,0:T(8,128)(2,1)} %bitcast.209), kind=kOutput, calls=%fused_computation.5 | convolution fusion | flops 1098899456 | bytes 72417280 | tf_op jit(solution)/shard_map/sqhd,skhd->shqk/dot_general | solution.py:68
  291.7 27.6 %multiply_convert_fusion.1 = bf16[2,16,256,1024]{3,2,1,0:T(8,128)(2,1)} fusion(f32[2,16,256,1024]{3,2,1,0:T(8,128)} %get-tuple-element.51, f32[2,16,256]{2,1,0:T(8,128)S(1)} %get-tuple-element.50, f32[2,16,256,1024]{3,2,1,0:T(8,128)} %get-tuple-element.43, f32[2,16,256]{2,1,0:T(8,128)S(1)} %get-tuple-element.42), kind=kLoop, calls=%fused_computation.4 | loop fusion | flops 33554432 | bytes 83951616 | tf_op jit(solution)/shard_map/convert_element_type | solution.py:80
  319.4 13.3 %multiply_convert_fusion.7 = bf16[2,16,64,256]{3,2,1,0:T(8,128)(2,1)} fusion(bf16[2,1024,16,64]{1,3,2,0:T(8,128)(2,1)} %bitcast.201, bf16[2,16,256,1024]{3,2,1,0:T(8,128)(2,1)} %multiply_convert_fusion.1), kind=kOutput, calls=%fused_computation.112 | convolution fusion | flops 1074790400 | bytes 22020096 | tf_op jit(solution)/shard_map/shqk,skhd->sqhd/dot_general | solution.py:82
  332.7 10.9 %multiply_convert_fusion.2 = bf16[2,16,64,1024]{3,2,1,0:T(8,128)(2,1)} fusion(bf16[2,256,16,64]{1,3,2,0:T(8,128)(2,1)S(1)} %bitcast.205, bf16[2,16,256,1024]{3,2,1,0:T(8,128)(2,1)} %multiply_convert_fusion.1), kind=kOutput, calls=%fused_computation.35 | convolution fusion | flops 1077936128 | bytes 22020096 | tf_op jit(solution)/shard_map/shqk,sqhd->skhd/dot_general | solution.py:88
  343.7 4.0 multiply_reduce_fusion.3
  347.7 6.2 copy.67
  354.6 2.9 fusion.152
  358.9 2.3 fusion.111
  361.2 2.1 copy.63
  363.3 23.7 %multiply_reduce_fusion = (f32[2,16,256]{2,1,0:T(8,128)S(1)}, f32[2,16,256,1024]{3,2,1,0:T(8,128)}) fusion(f32[2,16,256,1024]{3,2,1,0:T(8,128)} %get-tuple-element.39, f32[2,16,256]{2,1,0:T(8,128)S(1)} %copy-done.29, bf16[2,256,16,64]{1,3,2,0:T(8,128)(2,1)S(1)} %bitcast.214, bf16[2,1024,16,64]{1,3,2,0:T(8,128)(2,1)} %bitcast.207), kind=kOutput, calls=%fused_computation.3 | convolution fusion | flops 1098899456 | bytes 72417280 | tf_op jit(solution)/shard_map/sqhd,skhd->shqk/dot_general | solution.py:68
  387.0 27.9 %multiply_convert_fusion = bf16[2,16,256,1024]{3,2,1,0:T(8,128)(2,1)} fusion(f32[2,16,256,1024]{3,2,1,0:T(8,128)} %get-tuple-element.54, f32[2,16,256]{2,1,0:T(8,128)S(1)} %get-tuple-element.53, f32[2,16,256,1024]{3,2,1,0:T(8,128)} %get-tuple-element.39, f32[2,16,256]{2,1,0:T(8,128)S(1)} %copy-done.29), kind=kLoop, calls=%fused_computation.2 | loop fusion | flops 33554432 | bytes 83951616 | tf_op jit(solution)/shard_map/convert_element_type | solution.py:80
  414.9 10.8 %multiply_convert_fusion.3 = bf16[2,16,64,1024]{3,2,1,0:T(8,128)(2,1)} fusion(bf16[2,256,16,64]{1,3,2,0:T(8,128)(2,1)S(1)} %bitcast.203, bf16[2,16,256,1024]{3,2,1,0:T(8,128)(2,1)} %multiply_convert_fusion), kind=kOutput, calls=%fused_computation.36 | convolution fusion | flops 1077936128 | bytes 22020096 | tf_op jit(solution)/shard_map/shqk,sqhd->skhd/dot_general | solution.py:88
  425.6 6.2 copy.65
  433.1 16.6 %fusion.42 = bf16[2,16,64,1024]{3,2,1,0:T(8,128)(2,1)} fusion(bf16[2,256,16,64]{1,3,2,0:T(8,128)(2,1)S(1)} %bitcast.213, f32[2,16,256,1024]{3,2,1,0:T(8,128)} %get-tuple-element.43, f32[2,16,256]{2,1,0:T(8,128)S(1)} %get-tuple-element.42), kind=kOutput, calls=%fused_computation.69 | convolution fusion | flops 1092616192 | bytes 38830080 | tf_op jit(solution)/shard_map/shqk,sqhd->skhd/dot_general | solution.py:71
  449.7 6.2 copy.68
  457.1 14.7 %fusion.39 = bf16[2,16,64,1024]{3,2,1,0:T(8,128)(2,1)} fusion(bf16[2,256,16,64]{1,3,2,0:T(8,128)(2,1)S(1)} %bitcast.215, f32[2,16,256,1024]{3,2,1,0:T(8,128)} %get-tuple-element.39, f32[2,16,256]{2,1,0:T(8,128)S(1)} %copy-done.29), kind=kOutput, calls=%fused_computation.68 | convolution fusion | flops 1092616192 | bytes 38830080 | tf_op jit(solution)/shard_map/shqk,sqhd->skhd/dot_general | solution.py:71
  471.8 6.2 copy.66
  478.8 40.8 %all-reduce = (f32[3,1024]{1,0:T(4,128)}, f32[3,1024]{1,0:T(4,128)}) all-reduce(f32[3,1024]{1,0:T(4,128)S(1)} %get-tuple-element.55, f32[3,1024]{1,0:T(4,128)S(1)} %get-tuple-element.56), channel_id=1, replica_groups=mesh['dp'=8,'seq'=4] {'dp','seq'}, use_global_device_ids=true, to_apply=%region_27.28 | all-reduce | flops 6144 | bytes 49152 | tf_op jit(solution)/shard_map/psum | solution.py:225
  519.6 3.1 convolution_bitcast_fusion.1
  522.7 3.7 convolution_bitcast_fusion
  526.4 12.9 %multiply_convert_fusion.6 = bf16[2,16,64,256]{3,2,1,0:T(8,128)(2,1)S(1)} fusion(bf16[2,1024,16,64]{1,3,2,0:T(8,128)(2,1)} %bitcast.199, bf16[2,16,256,1024]{3,2,1,0:T(8,128)(2,1)} %multiply_convert_fusion), kind=kOutput, calls=%fused_computation.110 | convolution fusion | flops 1074790400 | bytes 22020096 | tf_op jit(solution)/shard_map/shqk,skhd->sqhd/dot_general | solution.py:82
  539.3 4.2 fusion.73
  543.6 4.6 fusion.53
  548.1 4.5 fusion.69
  552.6 4.8 add_convert_fusion.1
  557.4 14.4 %reduce-scatter.7.cloned.1.call-done = bf16[2,256,1024]{2,1,0:T(8,128)(2,1)} async-done(((bf16[2,1024,1024]{2,1,0:T(8,128)(2,1)}), bf16[2,256,1024]{2,1,0:T(8,128)(2,1)}) %reduce-scatter.7.cloned.1.call-update) | async-done | bytes 1048592 | tf_op jit(solution)/shard_map/reduce_scatter | solution.py:213
  571.8 6.1 add_convert_fusion.2
  577.9 141.8 %all-reduce.4.cloned.1.call-done = (f32[1024,512]{1,0:T(8,128)}, f32[512,1024]{1,0:T(8,128)}) async-done(((f32[1024,512]{1,0:T(8,128)}, f32[512,1024]{1,0:T(8,128)}), (f32[1024,512]{1,0:T(8,128)}, f32[512,1024]{1,0:T(8,128)})) %all-reduce.4.cloned.1.call-update) | async-done | bytes 4194320 | tf_op jit(solution)/shard_map/psum | solution.py:171
  719.7 3.2 copy.79
  (169 shorter events, 16.7 us)
Async XLA Ops:
  7.2 106.7 %copy-start = (bf16[1024,1024]{1,0:T(8,128)(2,1)S(1)}, bf16[1024,1024]{1,0:T(8,128)(2,1)}, u32[]{:S(2)}) copy-start(bf16[1024,1024]{1,0:T(8,128)(2,1)} %param.30) | copy-start | bytes 6291460
  7.2 4.5 copy-start.23
  7.2 41.7 %all-gather.7.cloned.1.call-start = ((), (), s32[]{:S(2)}) async-start(), calls=%async_computation.5 | async-start | bytes 5242880 | tf_op jit(solution)/shard_map/all_gather | solution.py:138
  11.6 74.0 %all-gather.5.cloned.1.call-start = ((), (), s32[]{:S(2)}) async-start(), calls=%async_computation.4 | async-start | bytes 5242880 | tf_op jit(solution)/shard_map/all_gather | solution.py:139
  15.5 106.8 %all-gather.11.cloned.1.call-start = ((), (), s32[]{:S(2)}) async-start(), calls=%async_computation.7 | async-start | bytes 5242880 | tf_op jit(solution)/shard_map/all_gather | solution.py:148
  19.7 139.0 %all-gather.9.cloned.1.call-start = ((), (), s32[]{:S(2)}) async-start(), calls=%async_computation.6 | async-start | bytes 5242880 | tf_op jit(solution)/shard_map/all_gather | solution.py:149
  24.2 519.4 %reduce-scatter.9.cloned.1.call-start = ((), (), s32[]{:S(2)}) async-start(), calls=%async_computation.10 | async-start | bytes 5242880 | tf_op jit(solution)/shard_map/reduce_scatter | solution.py:193
  24.3 6.1 copy-start.49
  24.3 6.1 copy-start.39
  24.3 6.7 copy-start.40
  24.3 7.3 %copy-start.50 = (s32[2]{0:T(128)S(1)}, s32[2]{0:T(128)}, u32[]{:S(2)}) copy-start(s32[2]{0:T(128)} %param.23) | copy-start | bytes 28
  24.3 7.4 %copy-start.56 = (s32[2]{0:T(128)S(1)}, s32[2]{0:T(128)}, u32[]{:S(2)}) copy-start(s32[2]{0:T(128)} %param.24) | copy-start | bytes 28
  30.1 25.0 %copy-start.6 = (bf16[2,256,1024]{1,2,0:T(8,128)(2,1)}, bf16[2,256,1024]{1,2,0:T(8,128)(2,1)S(1)}, u32[]{:S(2)}) copy-start(bf16[2,256,1024]{1,2,0:T(8,128)(2,1)S(1)} %copy.54) | copy-start | bytes 3145732
  31.0 148.9 %copy-start.37 = (f32[1,1024]{1,0:T(1,128)}, f32[1,1024]{1,0:T(1,128)S(1)}, u32[]{:S(2)}) copy-start(f32[1,1024]{1,0:T(1,128)S(1)} %get-tuple-element.31) | copy-start | bytes 12292
  74.2 17.6 %copy-start.28 = (f32[2,16,256]{2,1,0:T(8,128)}, f32[2,16,256]{2,1,0:T(8,128)S(1)}, u32[]{:S(2)}) copy-start(f32[2,16,256]{2,1,0:T(8,128)S(1)} %get-tuple-element.38) | copy-start | bytes 98308
  91.8 17.5 %copy-start.24 = (bf16[2,256,1024]{2,1,0:T(8,128)(2,1)S(1)}, bf16[2,256,1024]{2,1,0:T(8,128)(2,1)}, u32[]{:S(2)}) copy-start(bf16[2,256,1024]{2,1,0:T(8,128)(2,1)} %param.20) | copy-start | bytes 3145732
  112.6 1.3 copy-start.1
  112.6 67.3 %copy-start.30 = (f32[2,256]{1,0:T(2,128)}, f32[2,256]{1,0:T(2,128)S(1)}, u32[]{:S(2)}) copy-start(f32[2,256]{1,0:T(2,128)S(1)} %broadcast_multiply_fusion.2) | copy-start | bytes 6148
  113.0 0.9 copy-start.32
  113.9 66.1 %copy-start.41 = (f32[2,256]{1,0:T(2,128)}, f32[2,256]{1,0:T(2,128)S(1)}, u32[]{:S(2)}) copy-start(f32[2,256]{1,0:T(2,128)S(1)} %fusion.143) | copy-start | bytes 6148
  117.9 10.6 %copy-start.8 = (bf16[2,256,1024]{1,2,0:T(8,128)(2,1)}, bf16[2,256,1024]{1,2,0:T(8,128)(2,1)S(1)}, u32[]{:S(2)}) copy-start(bf16[2,256,1024]{1,2,0:T(8,128)(2,1)S(1)} %copy.58) | copy-start | bytes 3145732
  184.4 11.2 %copy-start.10 = (bf16[2,256,1024]{2,1,0:T(8,128)(2,1)}, bf16[2,256,1024]{2,1,0:T(8,128)(2,1)S(1)}, u32[]{:S(2)}) copy-start(bf16[2,256,1024]{2,1,0:T(8,128)(2,1)S(1)} %fusion.85) | copy-start | bytes 3145732
  184.4 11.2 %copy-start.54 = (bf16[1024,512]{1,0:T(8,128)(2,1)S(1)}, bf16[1024,512]{1,0:T(8,128)(2,1)}, u32[]{:S(2)}) copy-start(bf16[1024,512]{1,0:T(8,128)(2,1)} %param.36) | copy-start | bytes 3145732
  195.6 20.2 %copy-start.4 = (f32[2,256,4096]{2,1,0:T(8,128)}, f32[2,256,4096]{2,1,0:T(8,128)S(1)}, u32[]{:S(2)}) copy-start(f32[2,256,4096]{2,1,0:T(8,128)S(1)} %get-tuple-element.46) | copy-start | bytes 25165828
  195.6 2.0 copy-start.18
  215.8 11.9 %copy-start.5 = (f32[2,256,4096]{2,1,0:T(8,128)}, f32[2,256,4096]{2,1,0:T(8,128)S(1)}, u32[]{:S(2)}) copy-start(f32[2,256,4096]{2,1,0:T(8,128)S(1)} %fusion.10) | copy-start | bytes 25165828
  215.8 11.9 %copy-start.52 = (bf16[512,1024]{1,0:T(8,128)(2,1)S(1)}, bf16[512,1024]{1,0:T(8,128)(2,1)}, u32[]{:S(2)}) copy-start(bf16[512,1024]{1,0:T(8,128)(2,1)} %param.37) | copy-start | bytes 3145732
  215.9 11.9 %copy-start.57 = (f32[2]{0:T(128)S(1)}, f32[2]{0:T(128)}, u32[]{:S(2)}) copy-start(f32[2]{0:T(128)} %add_multiply_fusion) | copy-start | bytes 28
  227.8 3.1 copy-start.3
  227.8 3.1 copy-start.27
  230.9 3.1 copy-start.36
  235.8 14.8 %copy-start.17 = (bf16[2,256,1024]{2,1,0:T(8,128)(2,1)}, bf16[2,256,1024]{2,1,0:T(8,128)(2,1)S(1)}, u32[]{:S(2)}) copy-start(bf16[2,256,1024]{2,1,0:T(8,128)(2,1)S(1)} %get-tuple-element.28) | copy-start | bytes 3145732
  235.8 14.8 %copy-start.53 = (bf16[512,1024]{1,0:T(8,128)(2,1)S(1)}, bf16[512,1024]{1,0:T(8,128)(2,1)}, u32[]{:S(2)}) copy-start(bf16[512,1024]{1,0:T(8,128)(2,1)} %param.37) | copy-start | bytes 3145732
  235.8 14.8 %copy-start.59 = (f32[2,256,512]{2,1,0:T(8,128)S(1)}, f32[2,256,512]{2,1,0:T(8,128)}, u32[]{:S(2)}) copy-start(f32[2,256,512]{2,1,0:T(8,128)} %fusion.133) | copy-start | bytes 3145732
  250.7 2.2 copy-start.60
  252.9 7.4 %copy-start.26 = (bf16[2,256,512]{2,1,0:T(8,128)(2,1)}, bf16[2,256,512]{2,1,0:T(8,128)(2,1)S(1)}, u32[]{:S(2)}) copy-start(bf16[2,256,512]{2,1,0:T(8,128)(2,1)S(1)} %fusion.128) | copy-start | bytes 1572868
  252.9 7.4 %copy-start.55 = (bf16[1024,512]{1,0:T(8,128)(2,1)S(1)}, bf16[1024,512]{1,0:T(8,128)(2,1)}, u32[]{:S(2)}) copy-start(bf16[1024,512]{1,0:T(8,128)(2,1)} %param.36) | copy-start | bytes 3145732
  262.6 2.0 copy-start.51
  263.3 1.3 copy-start.15
  268.4 23.4 %copy-start.19 = (bf16[2,256,1024]{1,2,0:T(8,128)(2,1)}, bf16[2,256,1024]{1,2,0:T(8,128)(2,1)S(1)}, u32[]{:S(2)}) copy-start(bf16[2,256,1024]{1,2,0:T(8,128)(2,1)S(1)} %copy.61) | copy-start | bytes 3145732
  319.4 13.3 %copy-start.9 = (bf16[2,256,1024]{1,2,0:T(8,128)(2,1)S(1)}, bf16[2,256,1024]{1,2,0:T(8,128)(2,1)}, u32[]{:S(2)}) copy-start(bf16[2,256,1024]{1,2,0:T(8,128)(2,1)} %copy-done.8) | copy-start | bytes 3145732
  332.7 11.0 %copy-start.2 = (f32[2,256,1024]{2,1,0:T(8,128)S(1)}, f32[2,256,1024]{2,1,0:T(8,128)}, u32[]{:S(2)}) copy-start(f32[2,256,1024]{2,1,0:T(8,128)} %copy-done.1) | copy-start | bytes 6291460
  332.7 11.0 %copy-start.16 = (f32[2,256,1024]{2,1,0:T(8,128)S(1)}, f32[2,256,1024]{2,1,0:T(8,128)}, u32[]{:S(2)}) copy-start(f32[2,256,1024]{2,1,0:T(8,128)} %copy-done.15) | copy-start | bytes 6291460
  332.7 11.0 %copy-start.25 = (bf16[2,16,64,256]{3,2,1,0:T(8,128)(2,1)S(1)}, bf16[2,16,64,256]{3,2,1,0:T(8,128)(2,1)}, u32[]{:S(2)}) copy-start(bf16[2,16,64,256]{3,2,1,0:T(8,128)(2,1)} %multiply_convert_fusion.7) | copy-start | bytes 3145732
  332.7 11.0 %copy-start.31 = (f32[2,256]{1,0:T(2,128)S(1)}, f32[2,256]{1,0:T(2,128)}, u32[]{:S(2)}) copy-start(f32[2,256]{1,0:T(2,128)} %copy-done.30) | copy-start | bytes 6148
  332.7 11.0 %copy-start.38 = (f32[1,1024]{1,0:T(1,128)S(1)}, f32[1,1024]{1,0:T(1,128)}, u32[]{:S(2)}) copy-start(f32[1,1024]{1,0:T(1,128)} %copy-done.37) | copy-start | bytes 12292
  332.7 11.0 %copy-start.42 = (f32[2,256]{1,0:T(2,128)S(1)}, f32[2,256]{1,0:T(2,128)}, u32[]{:S(2)}) copy-start(f32[2,256]{1,0:T(2,128)} %copy-done.41) | copy-start | bytes 6148
  353.9 194.2 %reduce-scatter.5.cloned.1.call-start = ((), (), s32[]{:S(2)}) async-start(), calls=%async_computation.8 | async-start | bytes 5242880 | tf_op jit(solution)/shard_map/reduce_scatter | solution.py:210
  354.0 4.9 copy-start.12
  357.5 1.4 copy-start.13
  357.5 1.4 copy-start.47
  358.9 4.4 copy-start.29
  363.3 23.7 %copy-start.21 = (bf16[2,256,1024]{1,2,0:T(8,128)(2,1)}, bf16[2,256,1024]{1,2,0:T(8,128)(2,1)S(1)}, u32[]{:S(2)}) copy-start(bf16[2,256,1024]{1,2,0:T(8,128)(2,1)S(1)} %copy.63) | copy-start | bytes 3145732
  387.0 27.9 %copy-start.7 = (bf16[2,256,1024]{1,2,0:T(8,128)(2,1)S(1)}, bf16[2,256,1024]{1,2,0:T(8,128)(2,1)}, u32[]{:S(2)}) copy-start(bf16[2,256,1024]{1,2,0:T(8,128)(2,1)} %copy-done.6) | copy-start | bytes 3145732
  431.8 1.2 copy-start.20
  431.9 120.8 %reduce-scatter.11.cloned.1.call-start = ((), (), s32[]{:S(2)}) async-start(), calls=%async_computation.11 | async-start | bytes 5242880 | tf_op jit(solution)/shard_map/reduce_scatter | solution.py:196
  455.9 1.2 copy-start.22
  455.9 115.9 %reduce-scatter.7.cloned.1.call-start = ((), (), s32[]{:S(2)}) async-start(), calls=%async_computation.9 | async-start | bytes 5242880 | tf_op jit(solution)/shard_map/reduce_scatter | solution.py:213
  478.1 0.7 copy-start.45
  478.1 41.5 %copy-start.11 = (bf16[2,256,1024]{2,1,0:T(8,128)(2,1)S(1)}, bf16[2,256,1024]{2,1,0:T(8,128)(2,1)}, u32[]{:S(2)}) copy-start(bf16[2,256,1024]{2,1,0:T(8,128)(2,1)} %copy-done.10) | copy-start | bytes 3145732
  478.1 44.6 %copy-start.58 = (f32[2]{0:T(128)S(1)}, f32[2]{0:T(128)}, u32[]{:S(2)}) copy-start(f32[2]{0:T(128)} %add_multiply_fusion) | copy-start | bytes 28
  478.1 241.5 %all-reduce.4.cloned.1.call-start = ((), (), s32[]{:S(2)}) async-start(), calls=%async_computation.12 | async-start | bytes 8388608 | tf_op jit(solution)/shard_map/psum | solution.py:171
  552.6 19.2 %copy-start.48 = (f32[2,256]{1,0:T(2,128)S(1)}, f32[2,256]{1,0:T(2,128)}, u32[]{:S(2)}) copy-start(f32[2,256]{1,0:T(2,128)} %copy-done.47) | copy-start | bytes 6148
  719.7 3.2 copy-start.14
  (6 other events, 4.2 us)
Sparse Core Ops, SparseCore 0:
  11.7 37.1 all-gather.6
  51.1 34.4 all-gather.4
  87.7 34.4 all-gather.10
  124.2 34.4 all-gather.8
  354.0 44.5 reduce-scatter.8
  432.0 44.7 reduce-scatter.4
  479.3 45.2 reduce-scatter.10
  527.3 44.5 reduce-scatter.6
  577.6 142.0 all-reduce.3
where the time goes:
time: 737 us; the launch traced here: 731 us
  matrix products  319 us (43%)
  waiting for transfers between devices  200 us (27%)
  other arithmetic  85.4 us (12%)
  local copies, waits for them, and re-layouts  71.3 us (10%)
  blocking collectives  40.8 us (6%)
  between operations  14.7 us (2%)
    psum x1, waiting for transfers between devices, per_device(): lax.psum((adapter_down_grad, adapter_up_grad), ('dp', 'seq'))  142 us
    dot_general x12, matrix products, project_back(): jnp.einsum('ste,de->std', gradient, weight, preferred_element_type=jnp.fl...  58.2 us
    dot_general x12, matrix products, project(): jnp.einsum('std,de->ste', activation, weight, preferred_element_type=jnp....  57.6 us
    convert_element_type x2, other arithmetic, attend_back(): grad_low = grad_scores.astype(jnp.bfloat16)  55.5 us
    dot_general x2, matrix products, attend_back(): jnp.einsum('sqhd,skhd->shqk', grad_heads, split_heads(values), preferred_...  47.1 us
    psum x1, blocking collectives, per_device(): gain_grads, shift_grads = lax.psum((gain_grads, shift_grads), ('dp', 'seq'))  40.8 us
    sub x2, matrix products, attend(): weights = jnp.exp(scores - highest)  37.3 us
    dot_general x2, matrix products, attend(): jnp.einsum('shqk,skhd->sqhd', probabilities.astype(jnp.bfloat16), split_h...  32.4 us
  transfers between devices with their start and end apart: 9, of which 6 were waited for; matrix products, arithmetic and copies ran while one was open for 36% of the time, Pallas kernels for 0%

commit v1 on v0

v1 whole, which is shorter than its diff:
```python
import functools
import math

import jax
import jax.numpy as jnp
from jax import lax
from jax.experimental import pallas as pl
from jax.experimental.pallas import tpu as pltpu
from jax.sharding import PartitionSpec as P

HEAD_DIM = 64
PAIR = 2 * HEAD_DIM
EPS = 1e-05
NEGATIVE = -1e30
SCALE = HEAD_DIM ** (-0.5)
EXP2_SCALE = SCALE * math.log2(math.e)
HALF_LOG2E = 0.5 * math.log2(math.e)

f32 = jnp.float32
bf16 = jnp.bfloat16

NN = (((1,), (0,)), ((), ()))
NT = (((1,), (1,)), ((), ()))
TN = (((0,), (0,)), ((), ()))

ANY = pl.BlockSpec(memory_space=pl.ANY)
SMEM = pl.BlockSpec(memory_space=pltpu.SMEM)
VMEM = pl.BlockSpec(memory_space=pltpu.VMEM)
MIB = 2 ** 20


def dg(left, right, dims):
    return lax.dot_general(left, right, dims, preferred_element_type=f32)


def add(total, term):
    return term if total is None else total + term


def params(limit_mib):
    return pltpu.CompilerParams(vmem_limit_bytes=limit_mib * MIB)


def cost(flops, nbytes, exps=0):
    return pl.CostEstimate(flops=int(flops), bytes_accessed=int(nbytes), transcendentals=int(exps))


def shape(dims, dtype):
    return jax.ShapeDtypeStruct(dims, dtype)


def start_copies(pairs, sems):
    copies = [pltpu.make_async_copy(src, dst, sems.at[n]) for n, (src, dst) in enumerate(pairs)]
    for copy in copies:
        copy.start()
    return copies


def project_kernel(plan, n_in, *refs):
    count = len(plan)
    xs = refs[:n_in]
    ws = refs[n_in:n_in + count]
    n_out = 1 + max(o for _, o, _ in plan)
    outs = refs[n_in + count:n_in + count + n_out]
    held, sems = refs[n_in + count + n_out:]
    copies = start_copies([(w, held.at[j]) for j, w in enumerate(ws)], sems)
    for j, (i, o, row) in enumerate(plan):
        copies[j].wait()
        value = dg(xs[i][...], held[j], NN).astype(bf16)
        if row is None:
            outs[o][...] = value
        else:
            outs[o][row] = value


def project(xs, ws, plan, name):
    rows, width = xs[0].shape
    count = len(plan)
    n_out = 1 + max(o for _, o, _ in plan)
    out_shape = []
    for o in range(n_out):
        used = [row for _, oo, row in plan if oo == o]
        out_shape.append(shape((rows, width) if used[0] is None else (len(used), rows, width), bf16))
    return pl.pallas_call(
        functools.partial(project_kernel, plan, len(xs)),
        in_specs=[VMEM] * len(xs) + [ANY] * count,
        out_specs=[VMEM] * n_out,
        out_shape=out_shape,
        scratch_shapes=[pltpu.VMEM((count, width, width), bf16), pltpu.SemaphoreType.DMA((count,))],
        compiler_params=params(24),
        cost_estimate=cost(2 * count * rows * width * width, 2 * count * width * width),
        name=name,
    )(*xs, *ws)


def pair_masks():
    lane = lax.broadcasted_iota(jnp.int32, (1, PAIR), 1)
    return lane, lane < HEAD_DIM


def key_bias(start, length, rows):
    pos = start + lax.broadcasted_iota(jnp.int32, (rows, PAIR), 0)
    lane = lax.broadcasted_iota(jnp.int32, (rows, PAIR), 1)
    masked = jnp.where(pos < length, 0.0, NEGATIVE)
    return (
        jnp.where(lane == HEAD_DIM, masked, 0.0).astype(bf16),
        jnp.where(lane == 0, masked, 0.0).astype(bf16),
    )


def queries_with_one(q, half):
    one = jnp.ones((), bf16)
    return jnp.where(half, q, one), jnp.where(half, one, q)


def head_only(x, half):
    zero = jnp.zeros((), bf16)
    return jnp.where(half, x, zero), jnp.where(half, zero, x)


def soft(chunks, highest):
    probs = [jnp.exp2((s - highest) * EXP2_SCALE) for s in chunks]
    total = None
    for p in probs:
        total = add(total, p.sum(0, keepdims=True))
    return [p.astype(bf16) for p in probs], total


def top(chunks):
    highest = chunks[0].max(0, keepdims=True)
    for s in chunks[1:]:
        highest = jnp.maximum(highest, s.max(0, keepdims=True))
    return highest


def grad_columns(aT, oT, inverse):
    rows = aT.shape[1]
    sub = lax.broadcasted_iota(jnp.int32, (HEAD_DIM, rows), 0)
    zero = jnp.zeros((HEAD_DIM, rows), bf16)
    full, plain = [], []
    for h in range(2):
        sl = slice(h * HEAD_DIM, (h + 1) * HEAD_DIM)
        a = aT[sl].astype(f32) * inverse[h:h + 1]
        d = -(a * oT[sl].astype(f32)).sum(0, keepdims=True)
        high = d.astype(bf16).astype(f32)
        extra = jnp.where(sub == 0, high, jnp.where(sub == 1, d - high, 0.0)).astype(bf16)
        a = a.astype(bf16)
        full.append(jnp.concatenate([a, extra] if h == 0 else [extra, a], 0))
        plain.append(jnp.concatenate([a, zero] if h == 0 else [zero, a], 0))
    return full, plain


def values_with_ones(v, lane, half):
    first = jnp.where((lane == HEAD_DIM) | (lane == HEAD_DIM + 1), 1.0, 0.0).astype(bf16)
    second = jnp.where(lane < 2, 1.0, 0.0).astype(bf16)
    return jnp.where(half, v, first), jnp.where(half, second, v)


def cross_forward_kernel(n, sc_ref, q_ref, *refs):
    kvs = refs[:n]
    oT_ref, p_ref, inv_ref, bias_ref = refs[n:]
    rows = q_ref.shape[0]
    block = kvs[0].shape[1]
    lane, half = pair_masks()

    @pl.when(pl.program_id(0) == 0)
    def _():
        for j in range(n):
            bias_ref[0, j], bias_ref[1, j] = key_bias(sc_ref[1 + j], sc_ref[0], block)

    keys = [[], []]
    valuesT = []
    for j in range(n):
        k = kvs[j][0]
        keys[0].append(jnp.where(half, k, bias_ref[0, j]))
        keys[1].append(jnp.where(half, bias_ref[1, j], k))
        valuesT.append(kvs[j][1].T)
    queries = queries_with_one(q_ref[...], half)
    items = [(h, b) for b in range(rows // block) for h in range(2)]

    def score(item):
        h, b = item
        q = queries[h][b * block:(b + 1) * block]
        return [dg(keys[h][j], q, NT) for j in range(n)]

    later = score(items[0])
    for step, (h, b) in enumerate(items):
        chunks = later
        if step + 1 < len(items):
            later = score(items[step + 1])
        probs, total = soft(chunks, top(chunks))
        cols = pl.ds(b * block, block)
        out = None
        for j in range(n):
            p_ref[h, pl.ds(j * block, block), cols] = probs[j]
            out = add(out, dg(valuesT[j][h * HEAD_DIM:(h + 1) * HEAD_DIM], probs[j], NN))
        inverse = 1.0 / total
        inv_ref[0, pl.ds(h, 1), cols] = inverse
        oT_ref[pl.ds(h * HEAD_DIM, HEAD_DIM), cols] = (out * inverse).astype(bf16)


def feature_rows(rows):
    return pl.BlockSpec((PAIR, rows), lambda i: (i, 0))


def feature_cols(rows):
    return pl.BlockSpec((rows, PAIR), lambda i: (0, i))


def kv_cols(rows, count=2):
    return pl.BlockSpec((count, rows, PAIR), lambda i: (0, 0, i))


def pair_block(*dims):
    return pl.BlockSpec(dims, lambda i: (i,) + (0,) * (len(dims) - 1))


def cross_forward(scalars, q, kvs):
    n = len(kvs)
    rows, width = q.shape
    block = kvs[0].shape[1]
    pairs = width // PAIR
    every = n * block
    return pl.pallas_call(
        functools.partial(cross_forward_kernel, n),
        grid=(pairs,),
        in_specs=[SMEM, feature_cols(rows)] + [kv_cols(block)] * n,
        out_specs=[feature_rows(rows), pair_block(2, every, rows), pair_block(1, 2, rows)],
        out_shape=[
            shape((width, rows), bf16),
            shape((2 * pairs, every, rows), bf16),
            shape((pairs, 2, rows), f32),
        ],
        scratch_shapes=[pltpu.VMEM((2, n, block, PAIR), bf16)],
        compiler_params=params(32),
        cost_estimate=cost(16 * rows * every * width, 4 * pairs * every * rows, 2 * pairs * every * rows),
        name="cross_forward",
    )(scalars, q, *kvs)


def cross_backward_kernel(n, q_ref, p_ref, aT_ref, oT_ref, inv_ref, *refs):
    kvs = refs[:n]
    dqT_ref = refs[n]
    dkvs = refs[n + 1:]
    rows = q_ref.shape[0]
    block = kvs[0].shape[1]
    lane, half = pair_masks()
    values = [[], []]
    keysT = []
    for j in range(n):
        first, second = values_with_ones(kvs[j][1], lane, half)
        values[0].append(first)
        values[1].append(second)
        keysT.append(kvs[j][0].T)
    queries = head_only(q_ref[...], half)
    full, plain = grad_columns(aT_ref[...], oT_ref[...], inv_ref[0])
    items = [(h, b) for b in range(rows // block) for h in range(2)]

    def grad_probs(item):
        h, b = item
        a = full[h][:, b * block:(b + 1) * block]
        return [dg(values[h][j], a, NN) for j in range(n)]

    dk = [None] * n
    dv = [None] * n
    later = grad_probs(items[0])
    for step, (h, b) in enumerate(items):
        dps = later
        if step + 1 < len(items):
            later = grad_probs(items[step + 1])
        dq = None
        sl = slice(b * block, (b + 1) * block)
        for j in range(n):
            p = p_ref[h, pl.ds(j * block, block), pl.ds(b * block, block)]
            ds = (p * dps[j]).astype(bf16)
            dv[j] = add(dv[j], dg(p, plain[h][:, sl], NT))
            dk[j] = add(dk[j], dg(ds, queries[h][sl], NN))
            dq = add(dq, dg(keysT[j][h * HEAD_DIM:(h + 1) * HEAD_DIM], ds, NN))
        dqT_ref[pl.ds(h * HEAD_DIM, HEAD_DIM), pl.ds(b * block, block)] = (dq * SCALE).astype(bf16)
    for j in range(n):
        dkvs[j][0] = (dk[j] * SCALE).astype(bf16)
        dkvs[j][1] = dv[j].astype(bf16)


def cross_backward(q, probs, aT, oT, inverse, kvs):
    n = len(kvs)
    rows, width = q.shape
    block = kvs[0].shape[1]
    pairs = width // PAIR
    every = n * block
    return pl.pallas_call(
        functools.partial(cross_backward_kernel, n),
        grid=(pairs,),
        in_specs=[feature_cols(rows), pair_block(2, every, rows), feature_rows(rows), feature_rows(rows),
                  pair_block(1, 2, rows)] + [kv_cols(block)] * n,
        out_specs=[feature_rows(rows)] + [kv_cols(block)] * n,
        out_shape=[shape((width, rows), bf16)] + [shape((2, block, width), bf16)] * n,
        compiler_params=params(32),
        cost_estimate=cost(32 * rows * every * width, 4 * pairs * every * rows),
        name="cross_backward",
    )(q, probs, aT, oT, inverse, *kvs)


def self_forward_kernel(others, sc_ref, q_own, q_swap, *refs):
    kvs = refs[:2 + 2 * others]
    oT_ref, p_ref, inv_ref, tri_ref = refs[2 + 2 * others:]
    block = q_own.shape[0]
    lane, half = pair_masks()
    swapped = sc_ref[1] == 1

    @pl.when(pl.program_id(0) == 0)
    def _():
        key = lax.broadcasted_iota(jnp.int32, (block, block), 0)
        query = lax.broadcasted_iota(jnp.int32, (block, block), 1)
        tri_ref[...] = jnp.where(key <= query, 0.0, NEGATIVE)

    def low_high(first, second):
        return jnp.where(swapped, second, first), jnp.where(swapped, first, second)

    def prepare(k, start):
        bias = key_bias(start, sc_ref[0], block)
        return jnp.where(half, k, bias[0]), jnp.where(half, bias[1], k)

    q_low, q_high = low_high(q_own[...], q_swap[...])
    k_low, k_high = low_high(kvs[0][0], kvs[1][0])
    v_low, v_high = low_high(kvs[0][1], kvs[1][1])
    keys = [prepare(k_low, sc_ref[2]), prepare(k_high, sc_ref[3])]
    valuesT = [v_low.T, v_high.T]
    wraps = []
    for r in range(others):
        wrap = sc_ref[4 + 3 * r] == 1
        wraps.append(wrap)
        k_first, k_second = low_high(kvs[2 + 2 * r][0], kvs[3 + 2 * r][0])
        v_first, v_second = low_high(kvs[2 + 2 * r][1], kvs[3 + 2 * r][1])
        keys.append(prepare(k_first, sc_ref[5 + 3 * r]))
        keys.append(prepare(jnp.where(wrap, k_first, k_second), sc_ref[6 + 3 * r]))
        valuesT.append(v_first.T)
        valuesT.append(jnp.where(wrap, v_first, v_second).T)
    ones = [queries_with_one(q_low, half), queries_with_one(q_high, half)]
    either = [tuple(jnp.where(w, ones[0][h], ones[1][h]) for h in range(2)) for w in wraps]
    tri = tri_ref[...]

    def score(h):
        low = dg(keys[0][h], ones[0][h], NT) + tri
        high = [dg(keys[0][h], ones[1][h], NT), dg(keys[1][h], ones[1][h], NT) + tri]
        either_way = []
        for r in range(others):
            high.append(dg(keys[2 + 2 * r][h], ones[1][h], NT))
            either_way.append(dg(keys[3 + 2 * r][h], either[r][h], NT))
        return low, high, either_way

    later = score(0)
    for h in range(2):
        low, high, either_way = later
        if h == 0:
            later = score(1)
        top_low = low.max(0, keepdims=True)
        top_high = top(high)
        for r in range(others):
            peak = either_way[r].max(0, keepdims=True)
            top_low = jnp.where(wraps[r], jnp.maximum(top_low, peak), top_low)
            top_high = jnp.where(wraps[r], top_high, jnp.maximum(top_high, peak))
        p_low, sum_low = soft([low], top_low)
        p_high, sum_high = soft(high, top_high)
        sl = slice(h * HEAD_DIM, (h + 1) * HEAD_DIM)
        out_low = dg(valuesT[0][sl], p_low[0], NN)
        out_high = dg(valuesT[0][sl], p_high[0], NN) + dg(valuesT[1][sl], p_high[1], NN)
        p_ref[h, 0] = p_low[0]
        p_ref[h, 1] = p_high[0]
        p_ref[h, 2] = p_high[1]
        for r in range(others):
            p, total = soft([either_way[r]], jnp.where(wraps[r], top_low, top_high))
            out = dg(valuesT[3 + 2 * r][sl], p[0], NN)
            sum_low = jnp.where(wraps[r], sum_low + total, sum_low)
            sum_high = jnp.where(wraps[r], sum_high, sum_high + total)
            out_low = jnp.where(wraps[r], out_low + out, out_low)
            out_high = jnp.where(wraps[r], out_high, out_high + out)
            out_high = out_high + dg(valuesT[2 + 2 * r][sl], p_high[2 + r], NN)
            p_ref[h, 3 + 2 * r] = p_high[2 + r]
            p_ref[h, 4 + 2 * r] = p[0]
        inverse_low, inverse_high = 1.0 / sum_low, 1.0 / sum_high
        out_low, out_high = (out_low * inverse_low).astype(bf16), (out_high * inverse_high).astype(bf16)
        for n, value, inverse in ((0, out_low, inverse_low), (1, out_high, inverse_high)):
            inv_ref[0, n, pl.ds(h, 1), :] = inverse
        first, second = low_high(out_low, out_high)
        oT_ref[pl.ds(h * HEAD_DIM, HEAD_DIM), pl.ds(0, block)] = first
        oT_ref[pl.ds(h * HEAD_DIM, HEAD_DIM), pl.ds(block, block)] = second


def self_forward(scalars, q_own, q_swap, kvs):
    others = len(kvs) // 2 - 1
    block, width = q_own.shape
    pairs = width // PAIR
    tiles = 3 + 2 * others
    return pl.pallas_call(
        functools.partial(self_forward_kernel, others),
        grid=(pairs,),
        in_specs=[SMEM] + [feature_cols(block)] * 2 + [kv_cols(block)] * len(kvs),
        out_specs=[feature_rows(2 * block), pair_block(2, tiles, block, block), pair_block(1, 2, 2, block)],
        out_shape=[
            shape((width, 2 * block), bf16),
            shape((2 * pairs, tiles, block, block), bf16),
            shape((pairs, 2, 2, block), f32),
        ],
        scratch_shapes=[pltpu.VMEM((block, block), f32)],
        compiler_params=params(32),
        cost_estimate=cost(16 * tiles * block * block * width, 4 * pairs * tiles * block * block,
                           2 * pairs * tiles * block * block),
        name="self_forward",
    )(scalars, q_own, q_swap, *kvs)


def self_backward_kernel(others, sc_ref, q_own, q_swap, p_ref, aT_ref, oT_ref, inv_ref, *refs):
    kvs = refs[:2 + 2 * others]
    dqT_ref = refs[2 + 2 * others]
    dkvs = refs[3 + 2 * others:]
    block = q_own.shape[0]
    lane, half = pair_masks()
    swapped = sc_ref[1] == 1

    def low_high(first, second):
        return jnp.where(swapped, second, first), jnp.where(swapped, first, second)

    q_low, q_high = low_high(q_own[...], q_swap[...])
    k_low, k_high = low_high(kvs[0][0], kvs[1][0])
    v_low, v_high = low_high(kvs[0][1], kvs[1][1])
    keysT = [k_low.T, k_high.T]
    values = [values_with_ones(v_low, lane, half), values_with_ones(v_high, lane, half)]
    wraps = []
    for r in range(others):
        wrap = sc_ref[4 + 3 * r] == 1
        wraps.append(wrap)
        k_first, k_second = low_high(kvs[2 + 2 * r][0], kvs[3 + 2 * r][0])
        v_first, v_second = low_high(kvs[2 + 2 * r][1], kvs[3 + 2 * r][1])
        keysT.append(k_first.T)
        keysT.append(jnp.where(wrap, k_first, k_second).T)
        values.append(values_with_ones(v_first, lane, half))
        values.append(values_with_ones(jnp.where(wrap, v_first, v_second), lane, half))
    queries = [head_only(q_low, half), head_only(q_high, half)]
    a_low, a_high = low_high(aT_ref[:, 0:block], aT_ref[:, block:2 * block])
    o_low, o_high = low_high(oT_ref[:, 0:block], oT_ref[:, block:2 * block])
    grads = [grad_columns(a_low, o_low, inv_ref[0, 0]), grad_columns(a_high, o_high, inv_ref[0, 1])]
    tiles = [(0, 0, 0), (1, 0, 1), (2, 1, 1)]
    for r in range(others):
        tiles.append((3 + 2 * r, 2 + 2 * r, 1))
        tiles.append((4 + 2 * r, 3 + 2 * r, None))

    def side(tile, h, which):
        _, key, query = tile
        if query is not None:
            return queries[query][h] if which == 2 else grads[query][which][h]
        wrap = wraps[(key - 3) // 2]
        if which == 2:
            return jnp.where(wrap, queries[0][h], queries[1][h])
        return jnp.where(wrap, grads[0][which][h], grads[1][which][h])

    dk = [None] * len(keysT)
    dv = [None] * len(keysT)

    def grad_probs(h):
        return [dg(values[tile[1]][h], side(tile, h, 0), NN) for tile in tiles]

    later = grad_probs(0)
    for h in range(2):
        dps = later
        if h == 0:
            later = grad_probs(1)
        dq = [None, None]
        free = []
        for tile, dp in zip(tiles, dps):
            index, key, query = tile
            p = p_ref[h, index]
            ds = (p * dp).astype(bf16)
            dv[key] = add(dv[key], dg(p, side(tile, h, 1), NT))
            dk[key] = add(dk[key], dg(ds, side(tile, h, 2), NN))
            term = dg(keysT[key][h * HEAD_DIM:(h + 1) * HEAD_DIM], ds, NN)
            if query is None:
                free.append((wraps[(key - 3) // 2], term))
            else:
                dq[query] = add(dq[query], term)
        for wrap, term in free:
            dq = [jnp.where(wrap, dq[0] + term, dq[0]), jnp.where(wrap, dq[1], dq[1] + term)]
        first, second = low_high(dq[0], dq[1])
        dqT_ref[pl.ds(h * HEAD_DIM, HEAD_DIM), pl.ds(0, block)] = (first * SCALE).astype(bf16)
        dqT_ref[pl.ds(h * HEAD_DIM, HEAD_DIM), pl.ds(block, block)] = (second * SCALE).astype(bf16)

    def emit(n, row, low, high):
        first, second = low_high(low, high)
        dkvs[n][row] = first.astype(bf16)
        dkvs[n + 1][row] = second.astype(bf16)

    emit(0, 0, dk[0] * SCALE, dk[1] * SCALE)
    emit(0, 1, dv[0], dv[1])
    for r in range(others):
        wrap = wraps[r]
        for row, terms, factor in ((0, dk, SCALE), (1, dv, 1.0)):
            always, either = terms[2 + 2 * r] * factor, terms[3 + 2 * r] * factor
            emit(2 + 2 * r, row, jnp.where(wrap, always + either, always), jnp.where(wrap, 0.0, either))


def self_backward(scalars, q_own, q_swap, probs, aT, oT, inverse, kvs):
    others = len(kvs) // 2 - 1
    block, width = q_own.shape
    pairs = width // PAIR
    tiles = 3 + 2 * others
    return pl.pallas_call(
        functools.partial(self_backward_kernel, others),
        grid=(pairs,),
        in_specs=[SMEM] + [feature_cols(block)] * 2
        + [pair_block(2, tiles, block, block), feature_rows(2 * block), feature_rows(2 * block),
           pair_block(1, 2, 2, block)] + [kv_cols(block)] * len(kvs),
        out_specs=[feature_rows(2 * block)] + [kv_cols(block)] * len(kvs),
        out_shape=[shape((width, 2 * block), bf16)] + [shape((2, block, width), bf16)] * len(kvs),
        compiler_params=params(32),
        cost_estimate=cost(32 * tiles * block * block * width, 4 * pairs * tiles * block * block),
        name="self_backward",
    )(scalars, q_own, q_swap, probs, aT, oT, inverse, *kvs)


ROWS = 64


def normalized(z):
    center = z - jnp.mean(z, axis=-1, keepdims=True)
    spread = jnp.mean(center * center, axis=-1, keepdims=True)
    r = lax.rsqrt(spread + EPS)
    return center * r, r


def norm_back(G, n, r, gain):
    scaled = G * gain
    return r * (scaled - jnp.mean(scaled, -1, keepdims=True) - n * jnp.mean(scaled * n, -1, keepdims=True))


def spread_lanes(r):
    return jnp.broadcast_to(r, (r.shape[0], PAIR))


def for_rows(total, body, init=0):
    def step(i, carry):
        return body(pl.ds(pl.multiple_of(i * ROWS, ROWS), ROWS), carry)

    return lax.fori_loop(0, total // ROWS, step, init)


def fold(x):
    return x.reshape(x.shape[0] // 8, 8, x.shape[1]).sum(0)


def zero_sums(count, width):
    return tuple(jnp.zeros((8, width), f32) for _ in range(count))


def first_norm_kernel(oT_ref, x_own, x_swap, w_out, w_query, gain_ref, bias_ref, n_ref, r_ref, cq_ref,
                      held, low_ref, sems):
    copies = start_copies([(w_out, held.at[0]), (w_query, held.at[1])], sems)
    block = x_own.shape[0]
    rows = 2 * block
    copies[0].wait()
    n_ref[...] = dg(oT_ref[...], held[0], TN)
    gain, bias = gain_ref[0:1], bias_ref[0:1]
    for half, x_ref in enumerate((x_own, x_swap)):
        def body(sl, carry, half=half, x_ref=x_ref):
            rows_here = pl.ds(pl.multiple_of(sl.start + half * block, ROWS), ROWS)
            n, r = normalized(n_ref[rows_here] + x_ref[sl].astype(f32))
            n_ref[rows_here] = n
            r_ref[rows_here] = spread_lanes(r)
            low_ref[rows_here] = (n * gain + bias).astype(bf16)
            return carry
        for_rows(block, body)
    copies[1].wait()
    cq_ref[...] = dg(low_ref[...], held[1], NN).astype(bf16)


def first_norm(oT, x_own, x_swap, w_out, w_query, gain, bias):
    width, rows = oT.shape
    return pl.pallas_call(
        first_norm_kernel,
        in_specs=[VMEM] * 3 + [ANY] * 2 + [VMEM] * 2,
        out_specs=[VMEM] * 3,
        out_shape=[shape((rows, width), f32), shape((rows, PAIR), f32), shape((rows, width), bf16)],
        scratch_shapes=[pltpu.VMEM((2, width, width), bf16), pltpu.VMEM((rows, width), bf16),
                        pltpu.SemaphoreType.DMA((2,))],
        compiler_params=params(24),
        cost_estimate=cost(4 * rows * width * width, 4 * width * width + 10 * rows * width),
        name="first_norm",
    )(oT, x_own, x_swap, w_out, w_query, gain, bias)


def gelu_parts(x):
    gauss = jnp.exp2(x * x * (-HALF_LOG2E))
    t = 1.0 / (1.0 + (0.3275911 * math.sqrt(0.5)) * jnp.abs(x))
    poly = t * (0.254829592 + t * (-0.284496736 + t * (1.421413741 + t * (-1.453152027 + t * 1.061405429))))
    tail = 0.5 * poly * gauss
    phi = jnp.where(x >= 0.0, 1.0 - tail, tail)
    return x * phi, phi + x * gauss * (1.0 / math.sqrt(2.0 * math.pi))


def feed_forward_kernel(chunk, sc_ref, oT_ref, n1_ref, g_own, g_swap, w_out, w_in, w_back, w_down, w_up,
                        gain_ref, bias_ref,
                        out_own, out_swap, n2_ref, r2_ref, slope_ref, g3_ref, gai_ref, wg_ref, sums_ref,
                        out_w, in_w, back_w, down_w, up_w, low_ref, upd_ref, sems):
    block = g_own.shape[0]
    rows, width = n1_ref.shape
    hidden_units = w_in.shape[1]
    chunks = hidden_units // chunk
    adapter = w_down.shape[1]

    def in_copy(c):
        return pltpu.make_async_copy(
            w_in.at[:, pl.ds(pl.multiple_of(c * chunk, chunk), chunk)], in_w.at[c], sems.at[3 + c])

    def back_copy(c):
        return pltpu.make_async_copy(
            w_back.at[pl.ds(pl.multiple_of(c * chunk, chunk), chunk)], back_w.at[c], sems.at[3 + chunks + c])

    copies = start_copies([(w_out, out_w)], sems)
    for c in range(chunks):
        in_copy(c).start()
        back_copy(c).start()
        if c == 0:
            copies += [pltpu.make_async_copy(w_down, down_w, sems.at[1]),
                       pltpu.make_async_copy(w_up, up_w, sems.at[2])]
            copies[1].start()
            copies[2].start()

    gain1, bias1 = gain_ref[0:1], bias_ref[0:1]
    gain2, bias2 = gain_ref[1:2], bias_ref[1:2]
    gain3, bias3 = gain_ref[2:3], bias_ref[2:3]
    copies[0].wait()
    n2_ref[...] = dg(oT_ref[...], out_w[...], TN)

    def second(sl, carry):
        n, r = normalized(n2_ref[sl] + n1_ref[sl] * gain1 + bias1)
        n2_ref[sl] = n
        r2_ref[sl] = spread_lanes(r)
        low_ref[sl] = (n * gain2 + bias2).astype(bf16)
        return carry

    for_rows(rows, second)

    copies[1].wait()
    copies[2].wait()
    factor = (1.0 + sc_ref[0].astype(f32)) * 0.25
    adapter_in = dg(low_ref[...], down_w[...], NN)
    sig = 1.0 / (1.0 + jnp.exp(-adapter_in))
    adapter_hidden = (factor * (adapter_in * sig)).astype(bf16)
    adapter_slope = factor * (sig * (1.0 + adapter_in * (1.0 - sig)))
    upd_ref[...] = dg(adapter_hidden, up_w[...], NN)

    def step(c, carry):
        in_copy(c).wait()
        weight = in_w[c]
        parts = [dg(low_ref[pl.ds(b * block, block)], weight, NN) for b in range(2)]
        back_copy(c).wait()
        weight = back_w[c]
        cols = pl.ds(pl.multiple_of(c * chunk, chunk), chunk)
        for b in range(2):
            value, slope = gelu_parts(parts[b])
            slope_ref[pl.ds(b * block, block), cols] = slope.astype(bf16)
            upd_ref[pl.ds(b * block, block)] += dg(value.astype(bf16), weight, NN)
        return carry

    lax.fori_loop(0, chunks, step, 0)

    sums = zero_sums(2, width)
    for half, (g_ref, out_ref) in enumerate(((g_own, out_own), (g_swap, out_swap))):
        def third(sl, carry, half=half, g_ref=g_ref, out_ref=out_ref):
            here = pl.ds(pl.multiple_of(sl.start + half * block, ROWS), ROWS)
            n, r = normalized(n2_ref[here] * gain2 + bias2 + upd_ref[here])
            out_ref[sl] = (n * gain3 + bias3).astype(bf16)
            G = g_ref[sl].astype(f32)
            g3_ref[here] = norm_back(G, n, r, gain3)
            return carry[0] + fold(G * n), carry[1] + fold(G)
        sums = for_rows(block, third, sums)
    sums_ref[0:1] = sums[0].sum(0, keepdims=True)
    sums_ref[1:2] = sums[1].sum(0, keepdims=True)

    grad_update = g3_ref[...].astype(bf16)
    wg_ref[0:adapter] = dg(adapter_hidden, grad_update, TN).astype(wg_ref.dtype)
    gai = (adapter_slope * dg(grad_update, up_w[...], NT)).astype(bf16)
    gai_ref[...] = gai
    wg_ref[adapter:2 * adapter] = dg(gai, low_ref[...], TN).astype(wg_ref.dtype)


def feed_forward(scalars, oT, n1, g_own, g_swap, w_out, w_in, w_back, w_down, w_up, gain, bias):
    rows, width = n1.shape
    block = g_own.shape[0]
    units = w_in.shape[1]
    adapter = w_down.shape[1]
    chunk = 512
    chunks = units // chunk
    return pl.pallas_call(
        functools.partial(feed_forward_kernel, chunk),
        in_specs=[SMEM] + [VMEM] * 4 + [ANY] * 5 + [VMEM] * 2,
        out_specs=[VMEM] * 9,
        out_shape=[
            shape((block, width), bf16), shape((block, width), bf16), shape((rows, width), f32),
            shape((rows, PAIR), f32), shape((rows, units), bf16), shape((rows, width), f32),
            shape((rows, adapter), bf16), shape((2 * adapter, width), bf16), shape((2, width), f32),
        ],
        scratch_shapes=[
            pltpu.VMEM((width, width), bf16), pltpu.VMEM((chunks, width, chunk), bf16),
            pltpu.VMEM((chunks, chunk, width), bf16), pltpu.VMEM((width, adapter), bf16),
            pltpu.VMEM((adapter, width), bf16), pltpu.VMEM((rows, width), bf16),
            pltpu.VMEM((rows, width), f32), pltpu.SemaphoreType.DMA((3 + 2 * chunks,)),
        ],
        compiler_params=params(56),
        cost_estimate=cost(4 * rows * width * units + 12 * rows * width * adapter + 2 * rows * width * width,
                           4 * width * units, 2 * rows * units),
        name="feed_forward",
    )(scalars, oT, n1, g_own, g_swap, w_out, w_in, w_back, w_down, w_up, gain, bias)


def feed_back_kernel(chunk, g3_ref, slope_ref, gai_ref, n2_ref, r2_ref, w_in, w_back, w_down, w_out, gain_ref,
                     g2_ref, aT_ref, sums_ref, out_w, in_w, back_w, down_w, low_ref, sems):
    rows, width = g3_ref.shape
    chunks = w_in.shape[1] // chunk
    block = rows // 2

    def in_copy(c):
        return pltpu.make_async_copy(
            w_in.at[:, pl.ds(pl.multiple_of(c * chunk, chunk), chunk)], in_w.at[c], sems.at[2 + c])

    def back_copy(c):
        return pltpu.make_async_copy(
            w_back.at[pl.ds(pl.multiple_of(c * chunk, chunk), chunk)], back_w.at[c], sems.at[2 + chunks + c])

    copies = start_copies([(w_down, down_w)], sems)
    for c in range(chunks):
        back_copy(c).start()
        in_copy(c).start()
    copies.append(pltpu.make_async_copy(w_out, out_w, sems.at[1]))
    copies[1].start()
    low_ref[...] = g3_ref[...].astype(bf16)
    copies[0].wait()
    g2_ref[...] = g3_ref[...] + dg(gai_ref[...], down_w[...], NT)

    def step(c, carry):
        cols = pl.ds(pl.multiple_of(c * chunk, chunk), chunk)
        back_copy(c).wait()
        weight = back_w[c]
        parts = [dg(low_ref[pl.ds(b * block, block)], weight, NT) for b in range(2)]
        in_copy(c).wait()
        weight = in_w[c]
        for b in range(2):
            here = pl.ds(b * block, block)
            inner = (parts[b] * slope_ref[here, cols].astype(f32)).astype(bf16)
            g2_ref[here] += dg(inner, weight, NT)
        return carry

    lax.fori_loop(0, chunks, step, 0)
    gain2 = gain_ref[1:2]

    def second(sl, carry):
        G = g2_ref[sl]
        n = n2_ref[sl]
        grad = norm_back(G, n, r2_ref[sl][:, 0:1], gain2)
        g2_ref[sl] = grad
        low_ref[sl] = grad.astype(bf16)
        return carry[0] + fold(G * n), carry[1] + fold(G)

    sums = for_rows(rows, second, zero_sums(2, width))
    sums_ref[0:1] = sums[0].sum(0, keepdims=True)
    sums_ref[1:2] = sums[1].sum(0, keepdims=True)
    copies[1].wait()
    aT_ref[...] = dg(out_w[...], low_ref[...], NT).astype(bf16)


def feed_back(g3, slope, gai, n2, r2, w_in, w_back, w_down, w_out, gain):
    rows, width = g3.shape
    units = w_in.shape[1]
    adapter = w_down.shape[1]
    chunk = 512
    chunks = units // chunk
    return pl.pallas_call(
        functools.partial(feed_back_kernel, chunk),
        in_specs=[VMEM] * 5 + [ANY] * 4 + [VMEM],
        out_specs=[VMEM] * 3,
        out_shape=[shape((rows, width), f32), shape((width, rows), bf16), shape((2, width), f32)],
        scratch_shapes=[
            pltpu.VMEM((width, width), bf16), pltpu.VMEM((chunks, width, chunk), bf16),
            pltpu.VMEM((chunks, chunk, width), bf16), pltpu.VMEM((width, adapter), bf16),
            pltpu.VMEM((rows, width), bf16), pltpu.SemaphoreType.DMA((2 + 2 * chunks,)),
        ],
        compiler_params=params(52),
        cost_estimate=cost(4 * rows * width * units + 2 * rows * width * adapter + 2 * rows * width * width,
                           4 * width * units),
        name="feed_back",
    )(g3, slope, gai, n2, r2, w_in, w_back, w_down, w_out, gain)


def first_back_kernel(g2_ref, dqT_ref, n_ref, r_ref, w_query, w_out, gain_ref, g1_ref, aT_ref, sums_ref,
                      held, low_ref, sems):
    copies = start_copies([(w_query, held.at[0]), (w_out, held.at[1])], sems)
    rows, width = g2_ref.shape
    dq = dqT_ref[...].T
    copies[0].wait()
    g1_ref[...] = g2_ref[...] + dg(dq, held[0], NT)
    gain = gain_ref[0:1]

    def body(sl, carry):
        G = g1_ref[sl]
        n = n_ref[sl]
        grad = norm_back(G, n, r_ref[sl][:, 0:1], gain)
        g1_ref[sl] = grad
        low_ref[sl] = grad.astype(bf16)
        return carry[0] + fold(G * n), carry[1] + fold(G)

    sums = for_rows(rows, body, zero_sums(2, width))
    sums_ref[0:1] = sums[0].sum(0, keepdims=True)
    sums_ref[1:2] = sums[1].sum(0, keepdims=True)
    copies[1].wait()
    aT_ref[...] = dg(held[1], low_ref[...], NT).astype(bf16)


def first_back(g2, dqT, n1, r1, w_query, w_out, gain):
    rows, width = g2.shape
    return pl.pallas_call(
        first_back_kernel,
        in_specs=[VMEM] * 4 + [ANY] * 2 + [VMEM],
        out_specs=[VMEM] * 3,
        out_shape=[shape((rows, width), f32), shape((width, rows), bf16), shape((2, width), f32)],
        scratch_shapes=[pltpu.VMEM((2, width, width), bf16), pltpu.VMEM((rows, width), bf16),
                        pltpu.SemaphoreType.DMA((2,))],
        compiler_params=params(28),
        cost_estimate=cost(4 * rows * width * width, 4 * width * width + 10 * rows * width),
        name="first_back",
    )(g2, dqT, n1, r1, w_query, w_out, gain)


def key_grad_kernel(others, *refs):
    mine = refs[0]
    received = refs[1:1 + others]
    w_key, w_value, out_ref, held, sems = refs[1 + others:]
    copies = start_copies([(w_key, held.at[0]), (w_value, held.at[1])], sems)
    total = None
    for n in range(2):
        part = mine[n].astype(f32)
        for ref in received:
            part = part + ref[n].astype(f32)
        part = part.astype(bf16)
        copies[n].wait()
        total = add(total, dg(part, held[n], NT))
    out_ref[...] = total.astype(bf16)


def key_grad(mine, received, w_key, w_value):
    _, block, width = mine.shape
    others = len(received)
    return pl.pallas_call(
        functools.partial(key_grad_kernel, others),
        in_specs=[VMEM] * (1 + others) + [ANY] * 2,
        out_specs=VMEM,
        out_shape=shape((block, width), bf16),
        scratch_shapes=[pltpu.VMEM((2, width, width), bf16), pltpu.SemaphoreType.DMA((2,))],
        compiler_params=params(20),
        cost_estimate=cost(4 * block * width * width, 4 * width * width),
        name="enc_grad",
    )(mine, *received, w_key, w_value)


def token_grad_kernel(others, half, *refs):
    g1_ref, dqT_ref, mine = refs[:3]
    received = refs[3:3 + others]
    w_query, w_key, w_value, out_ref, held, sems = refs[3 + others:]
    copies = start_copies([(w, held.at[n]) for n, w in enumerate((w_query, w_key, w_value))], sems)
    block = out_ref.shape[0]
    rows = pl.ds(half * block, block)
    dq = dqT_ref[:, rows].T
    copies[0].wait()
    total = g1_ref[rows] + dg(dq, held[0], NT)
    for n in range(2):
        part = mine[n].astype(f32)
        for ref in received:
            part = part + ref[n].astype(f32)
        part = part.astype(bf16)
        copies[n + 1].wait()
        total = total + dg(part, held[n + 1], NT)
    out_ref[...] = total.astype(bf16)


def token_grad(half, g1, dqT, mine, received, w_query, w_key, w_value):
    _, block, width = mine.shape
    others = len(received)
    return pl.pallas_call(
        functools.partial(token_grad_kernel, others, half),
        in_specs=[VMEM] * (3 + others) + [ANY] * 3,
        out_specs=VMEM,
        out_shape=shape((block, width), bf16),
        scratch_shapes=[pltpu.VMEM((3, width, width), bf16), pltpu.SemaphoreType.DMA((3,))],
        compiler_params=params(24),
        cost_estimate=cost(6 * block * width * width, 6 * width * width),
        name="token_grad",
    )(g1, dqT, mine, *received, w_query, w_key, w_value)


def exchange_bits(x, axis, bit):
    return lax.ppermute(x, axis, [(i, i ^ bit) for i in range(lax.axis_size(axis))])


def reduce_everywhere(x, steps):
    for axis, bit in steps:
        mine = (lax.axis_index(axis) // bit) % 2
        half = x.shape[0] // 2
        send = lax.dynamic_slice_in_dim(x, (1 - mine) * half, half, 0)
        keep = lax.dynamic_slice_in_dim(x, mine * half, half, 0)
        x = (keep.astype(f32) + exchange_bits(send, axis, bit).astype(f32)).astype(bf16)
    for axis, bit in reversed(steps):
        mine = (lax.axis_index(axis) // bit) % 2
        other = exchange_bits(x, axis, bit)
        x = jnp.where(mine == 1, jnp.concatenate([other, x]), jnp.concatenate([x, other]))
    return x


def bits(size):
    return [1 << n for n in range(size.bit_length() - 1)]


def per_device(
    tokens, enc_states, dec_lengths, enc_lengths, adapter_step, out_grad,
    self_query, self_key, self_value, self_out, cross_query, cross_key, cross_value, cross_out,
    ffn_in, ffn_out, adapter_down, adapter_up, ln_gain, ln_bias,
):
    group = lax.axis_size("seq")
    half = group // 2
    others = half - 1
    member = lax.axis_index("seq")
    side = member // half
    block = tokens.shape[1]
    low = jnp.where(side == 1, group - 1 - member, member)
    swap = [(i, group - 1 - i) for i in range(group)]

    def place(s, index):
        return group - 1 - index if s == 1 else index

    def from_shift(r):
        return [(place(s, (i + r) % half), place(s, i)) for s in range(2) for i in range(half)]

    def to_shift(r):
        return [(place(s, i), place(s, (i + r) % half)) for s in range(2) for i in range(half)]

    def split(x):
        mine = lax.dynamic_index_in_dim(x, side, 0, keepdims=False)
        theirs = lax.dynamic_index_in_dim(x, 1 - side, 0, keepdims=False)
        return mine, lax.ppermute(theirs, "seq", swap)

    def joined(mine, theirs):
        back = lax.ppermute(theirs, "seq", swap)
        return jnp.where(side == 1, jnp.stack([back, mine]), jnp.stack([mine, back]))

    dec_length = dec_lengths[side]
    enc_length = enc_lengths[side]
    x_own, x_swap = split(tokens)
    e_own, e_swap = split(enc_states)
    g_own, g_swap = split(out_grad)

    def starts(index):
        own = jnp.where(side == 1, group - 1 - index, index)
        return own * block, (group - 1 - own) * block

    self_scalars = [dec_length, side, low * block, (group - 1 - low) * block]
    cross_scalars = [enc_length, *starts(low)]
    for r in range(1, half):
        index = (low + r) % half
        wrap = low + r >= half
        first = index * block
        second = (group - 1 - index) * block
        self_scalars += [wrap.astype(jnp.int32), first, jnp.where(wrap, first, second)]
        cross_scalars += [*starts(index)]
    self_scalars = jnp.stack([jnp.asarray(s, jnp.int32) for s in self_scalars])
    cross_scalars = jnp.stack([jnp.asarray(s, jnp.int32) for s in cross_scalars])

    q_own, kv_own, ckv_own = project(
        [x_own, e_own], [self_key, self_value, self_query, cross_key, cross_value],
        ((0, 1, 0), (0, 1, 1), (0, 0, None), (1, 2, 0), (1, 2, 1)), "project_own")
    kv_swap, q_swap = project(
        [x_swap], [self_key, self_value, self_query], ((0, 0, 0), (0, 0, 1), (0, 1, None)), "project_swap")
    ckv_swap, = project([e_swap], [cross_key, cross_value], ((0, 0, 0), (0, 0, 1)), "project_enc")

    def gathered(own, swapped):
        every = [own, swapped]
        for r in range(1, half):
            every += [lax.ppermute(own, "seq", from_shift(r)), lax.ppermute(swapped, "seq", from_shift(r))]
        return every

    kvs = gathered(kv_own, kv_swap)
    oT, probs, inverse = self_forward(self_scalars, q_own, q_swap, kvs)
    n1, r1, cq = first_norm(oT, x_own, x_swap, self_out, cross_query, ln_gain, ln_bias)
    ckvs = gathered(ckv_own, ckv_swap)
    coT, cprobs, cinverse = cross_forward(cross_scalars, cq, ckvs)
    step_of = adapter_step[side][None]
    out_own, out_swap, n2, r2, slope, g3, gai, weight_grads, sums3 = feed_forward(
        step_of, coT, n1, g_own, g_swap, cross_out, ffn_in, ffn_out, adapter_down, adapter_up, ln_gain, ln_bias)
    layer_output = joined(out_own, out_swap)

    seq_bits, dp_bits = bits(group), bits(lax.axis_size("dp"))
    steps = [("seq", seq_bits[0])] + [("dp", b) for b in dp_bits] + [("seq", b) for b in seq_bits[1:]]
    weight_grads = reduce_everywhere(weight_grads, steps)
    adapter = adapter_down.shape[1]
    adapter_up_grad = weight_grads[:adapter].astype(f32)
    adapter_down_grad = weight_grads[adapter:].astype(f32).T

    g2, caT, sums2 = feed_back(g3, slope, gai, n2, r2, ffn_in, ffn_out, adapter_down, cross_out, ln_gain)
    cdqT, *cdkvs = cross_backward(cq, cprobs, caT, coT, cinverse, ckvs)

    def returned(parts):
        own, swapped = [], []
        for r in range(1, half):
            own.append(lax.ppermute(parts[2 * r], "seq", to_shift(r)))
            swapped.append(lax.ppermute(parts[2 * r + 1], "seq", to_shift(r)))
        return own, swapped

    enc_back = returned(cdkvs)
    enc_swap = key_grad(cdkvs[1], enc_back[1], cross_key, cross_value)
    enc_own = key_grad(cdkvs[0], enc_back[0], cross_key, cross_value)
    enc_grad = joined(enc_own, enc_swap)

    g1, aT, sums1 = first_back(g2, cdqT, n1, r1, cross_query, self_out, ln_gain)
    sums = jnp.concatenate([sums1, sums2, sums3])
    sums = jnp.sum(lax.all_gather(sums, ("dp", "seq")), 0)
    dqT, *dkvs = self_backward(self_scalars, q_own, q_swap, probs, aT, oT, inverse, kvs)
    token_back = returned(dkvs)
    t_swap = token_grad(1, g1, dqT, dkvs[1], token_back[1], self_query, self_key, self_value)
    t_own = token_grad(0, g1, dqT, dkvs[0], token_back[0], self_query, self_key, self_value)
    return (
        layer_output,
        joined(t_own, t_swap),
        enc_grad,
        adapter_down_grad,
        adapter_up_grad,
        sums[0::2],
        sums[1::2],
    )


def solution(mesh):
    rows = P("dp", "seq", None)
    return jax.shard_map(
        per_device,
        mesh=mesh,
        in_specs=(rows, rows, P("dp"), P("dp"), P("dp"), rows) + (P(),) * 14,
        out_specs=(rows, rows, rows, P(), P(), P(), P()),
        check_vma=False,
    )
```

time: 737 us -> 359 us (0.49)
  matrix products: 319 us -> 0 us
  Pallas kernels: 0 us -> 168 us
  waiting for transfers between devices: 200 us -> 51.5 us
  other arithmetic: 85.4 us -> 22.1 us
  local copies, waits for them, and re-layouts: 71.3 us -> 41.5 us
  starting transfers between devices: 0.37 us -> 23.3 us
  between operations: 14.7 us -> 1.43 us
    dot_general x36 -> x0, matrix products: 281 us -> none  [the longest x12 58.2 us: project_back(): jnp.einsum('ste,de->std', gradient, weight, preferred_element_type=jnp.fl...]
    pallas_call x0 -> x15, Pallas kernels: none -> 168 us  [the longest x1 33.2 us: feed_forward(): pl.pallas_call(functools.partial(feed_forward_kernel, chunk), in_specs=[S...]
    psum x1 -> x0, waiting for transfers between devices: 142 us -> none  [per_device(): lax.psum((adapter_down_grad, adapter_up_grad), ('dp', 'seq'))]
    ppermute x0 -> x24, waiting for transfers between devices: none -> 51.5 us  [the longest x10 35.2 us: exchange_bits(): lax.ppermute(x, axis, [(i, i ^ bit) for i in range(lax.axis_size(axis))])]
    convert_element_type x4 -> x6, other arithmetic: 57.7 us -> 8.66 us  [the longest x5 6.21 us: reduce_everywhere(): (keep.astype(f32) + exchange_bits(send, axis, bit).astype(f32)).astype(bf16)]
    all_gather x0 -> x1, blocking collectives: none -> 46.6 us  [per_device(): sums = jnp.sum(lax.all_gather(sums, ('dp', 'seq')), 0)]
    all_gather x4 -> x0, waiting for transfers between devices: 43.4 us -> none  [the longest x1 15.6 us: per_device(): lax.all_gather(own_keys, 'seq', axis=1, tiled=True)]
    psum x1 -> x0, blocking collectives: 40.8 us -> none  [per_device(): gain_grads, shift_grads = lax.psum((gain_grads, shift_grads), ('dp', 'seq'))]
  transfers between devices with their start and end apart: 9 -> 24, of which waited for: 6 -> 9; matrix products, arithmetic and copies ran while one was open for 36% -> 5% of each run, Pallas kernels for 0% -> 38%
where the time goes in v1:
time: 359 us; the launch traced here: 355 us
  Pallas kernels  168 us (47%)
  waiting for transfers between devices  51.5 us (14%)
  blocking collectives  46.6 us (13%)
  local copies, waits for them, and re-layouts  41.5 us (12%)
  starting transfers between devices  23.3 us (6%)
  other arithmetic  22.1 us (6%)
    all_gather x1, blocking collectives, per_device(): sums = jnp.sum(lax.all_gather(sums, ('dp', 'seq')), 0)  46.6 us
    ppermute x10, waiting for transfers between devices, exchange_bits(): lax.ppermute(x, axis, [(i, i ^ bit) for i in range(lax.axis_size(axis))])  35.2 us
    pallas_call x1, Pallas kernels, feed_forward(): pl.pallas_call(functools.partial(feed_forward_kernel, chunk), in_specs=[S...  33.2 us
    unnamed x119, local copies, waits for them, and re-layouts  30.4 us
    pallas_call x1, Pallas kernels, feed_back(): pl.pallas_call(functools.partial(feed_back_kernel, chunk), in_specs=[VMEM...  20.7 us
    pallas_call x1, Pallas kernels, cross_backward(): pl.pallas_call(functools.partial(cross_backward_kernel, n), grid=(pairs,)...  19.9 us
    pallas_call x1, Pallas kernels, cross_forward(): pl.pallas_call(functools.partial(cross_forward_kernel, n), grid=(pairs,),...  18.7 us
    pallas_call x1, Pallas kernels, first_back(): pl.pallas_call(first_back_kernel, in_specs=[VMEM] * 4 + [ANY] * 2 + [VMEM...  16.2 us
  transfers between devices with their start and end apart: 24, of which 9 were waited for; matrix products, arithmetic and copies ran while one was open for 5% of the time, Pallas kernels for 38%

profile of v1, /device:TPU:0, one launch (start us, length us, event | category | flops | bytes accessed | tf_op | source)
XLA Modules:
  0.0 354.9 jit_solution(11863189550859225907)
XLA Ops:
  0.7 1.4 dynamic-slice_bitcast_fusion.3
  2.1 2.5 collective-permute-start
  4.6 1.3 dynamic-slice_bitcast_fusion.2
  5.9 1.6 copy-done.4
  7.5 1.6 copy-done.7
  9.1 1.6 copy-done.10
  10.7 5.3 %project_own.1 = (bf16[256,1024]{1,0:T(8,128)(2,1)S(1)}, bf16[2,256,1024]{2,1,0:T(8,128)(2,1)}, bf16[2,256,1024]{2,1,0:T(8,128)(2,1)}) custom-call(bf16[256,1024]{1,0:T(8,128)(2,1)S(1)} %get-tuple-element.106.refs_0_.x_own, bf16[256,1024]{1,0:T(8,128)(2,1)S(1)} %get-tuple-element.104.refs_1_, bf16[1024,1024]{1,0:T(8,128)(2,1)S(1)} %copy-done.4, ...), custom_call_target="tpu_custom_call" | custom-call | flops 2684354560 | bytes 10485760 | tf_op jit(solution)/shard_map/project_own/pallas_call | solution.py:84
  16.9 2.8 project_swap.1
  19.9 2.5 collective-permute-start.3
  22.6 12.0 %collective-permute-done.3.refs_0_ = bf16[256,1024]{1,0:T(8,128)(2,1)S(1)} collective-permute-done((bf16[256,1024]{1,0:T(8,128)(2,1)S(1)}, bf16[256,1024]{1,0:T(8,128)(2,1)S(1)}, u32[]{:S(2)}, u32[]{:S(2)}) %collective-permute-start.3) | collective-permute-done | bytes 524320 | tf_op jit(solution)/shard_map/ppermute | solution.py:946
  34.6 2.7 project_enc.1.refs_1_
  37.5 1.0 dynamic-slice_bitcast_fusion
  38.6 1.6 collective-permute-start.6
  43.6 1.0 copy-done.35
  44.6 1.0 copy-done.38
  45.6 13.1 %self_forward.1 = (bf16[1024,512]{1,0:T(8,128)(2,1)S(1)}, bf16[16,5,256,256]{3,2,1,0:T(8,128)(2,1)S(1)}, f32[8,2,2,256]{3,2,1,0:T(2,128)S(1)}) custom-call(s32[7]{0:T(128)S(1)} %stack.93.sc_ref, bf16[256,1024]{1,0:T(8,128)(2,1)S(1)} %copy-done.35, bf16[256,1024]{1,0:T(8,128)(2,1)S(1)} %copy-done.38, bf16[2,256,1024]{2,1,0:T(8,128)(2,1)} %get-tuple-element.48.refs_0_, ...), custom_call_target="tpu_custom_call" | custom-call | flops 5368709120 | bytes 10485760 | tf_op jit(solution)/shard_map/self_forward/pallas_call | solution.py:395
  58.8 4.0 %copy-done.45 = bf16[16,5,256,256]{3,2,1,0:T(8,128)(2,1)} copy-done((bf16[16,5,256,256]{3,2,1,0:T(8,128)(2,1)}, bf16[16,5,256,256]{3,2,1,0:T(8,128)(2,1)S(1)}, u32[]{:S(2)}) %copy-start.45) | copy-done | bytes 10485784
  62.8 4.6 %first_norm.1 = (f32[512,1024]{1,0:T(8,128)S(1)}, f32[512,128]{1,0:T(8,128)S(1)}, bf16[512,1024]{1,0:T(8,128)(2,1)S(1)}) custom-call(bf16[1024,512]{1,0:T(8,128)(2,1)S(1)} %get-tuple-element.50.oT_ref, bf16[256,1024]{1,0:T(8,128)(2,1)S(1)} %get-tuple-element.106.refs_0_.x_own, bf16[256,1024]{1,0:T(8,128)(2,1)S(1)} %collective-permute-done.refs_0_.x_swap, ...), custom_call_target="tpu_custom_call" | custom-call | flops 2147483648 | bytes 9437184 | tf_op jit(solution)/shard_map/first_norm/pallas_call | solution.py:577
  67.4 1.3 copy-done.20
  68.8 18.7 %cross_forward.1 = (bf16[1024,512]{1,0:T(8,128)(2,1)S(1)}, bf16[16,1024,512]{2,1,0:T(8,128)(2,1)}, f32[8,2,512]{2,1,0:T(2,128)S(1)}) custom-call(s32[5]{0:T(128)S(1)} %stack.85.sc_ref, bf16[512,1024]{1,0:T(8,128)(2,1)S(1)} %get-tuple-element.51.q_ref, bf16[2,256,1024]{2,1,0:T(8,128)(2,1)} %get-tuple-element.52.refs_0_, ...), custom_call_target="tpu_custom_call" | custom-call | flops 8589934592 | bytes 16777216 | tf_op jit(solution)/shard_map/cross_forward/pallas_call | solution.py:224
  88.5 33.2 %feed_forward.1 = (bf16[256,1024]{1,0:T(8,128)(2,1)}, bf16[256,1024]{1,0:T(8,128)(2,1)}, f32[512,1024]{1,0:T(8,128)}, f32[512,128]{1,0:T(8,128)}, bf16[512,4096]...) custom-call(s32[1]{0:T(128)} %dynamic_slice.58.sc_ref, ...), custom_call_target="tpu_custom_call" | custom-call | flops 12884901888 | bytes 16777216 | tf_op jit(solution)/shard_map/feed_forward/pallas_call | solution.py:693
  121.7 1.3 constant_dynamic-slice_fusion.4
  123.4 2.5 collective-permute-done.14
  125.9 1.9 add_convert_fusion
  129.6 1.4 collective-permute-start.15
  131.0 13.0 %collective-permute-done.15 = bf16[256,1024]{1,0:T(8,128)(2,1)} collective-permute-done((bf16[256,1024]{1,0:T(8,128)(2,1)}, bf16[256,1024]{1,0:T(8,128)(2,1)}, u32[]{:S(2)}, u32[]{:S(2)}) %collective-permute-start.15) | collective-permute-done | bytes 524320 | tf_op jit(solution)/shard_map/ppermute | solution.py:899
  144.1 1.4 add_convert_fusion.1
  146.3 1.6 collective-permute-start.16
  147.9 6.2 %collective-permute-done.16 = bf16[128,1024]{1,0:T(8,128)(2,1)} collective-permute-done((bf16[128,1024]{1,0:T(8,128)(2,1)S(1)}, bf16[128,1024]{1,0:T(8,128)(2,1)}, u32[]{:S(2)}, u32[]{:S(2)}) %collective-permute-start.16) | collective-permute-done | bytes 262176 | tf_op jit(solution)/shard_map/ppermute | solution.py:899
  154.1 1.1 add_convert_fusion.2
  155.9 2.6 collective-permute-start.17
  158.5 5.4 %collective-permute-done.17 = bf16[64,1024]{1,0:T(8,128)(2,1)} collective-permute-done((bf16[64,1024]{1,0:T(8,128)(2,1)}, bf16[64,1024]{1,0:T(8,128)(2,1)}, u32[]{:S(2)}, u32[]{:S(2)}) %collective-permute-start.17) | collective-permute-done | bytes 131104 | tf_op jit(solution)/shard_map/ppermute | solution.py:899
  166.0 4.1 %collective-permute-done.18 = bf16[32,1024]{1,0:T(8,128)(2,1)S(1)} collective-permute-done((bf16[32,1024]{1,0:T(8,128)(2,1)S(1)}, bf16[32,1024]{1,0:T(8,128)(2,1)S(1)}, u32[]{:S(2)}, u32[]{:S(2)}) %collective-permute-start.18) | collective-permute-done | bytes 65568 | tf_op jit(solution)/shard_map/ppermute | solution.py:899
  171.3 3.9 %collective-permute-done.19 = bf16[32,1024]{1,0:T(8,128)(2,1)S(1)} collective-permute-done((bf16[32,1024]{1,0:T(8,128)(2,1)S(1)}, bf16[32,1024]{1,0:T(8,128)(2,1)S(1)}, u32[]{:S(2)}, u32[]{:S(2)}) %collective-permute-start.19) | collective-permute-done | bytes 65568 | tf_op jit(solution)/shard_map/ppermute | solution.py:899
  176.2 20.7 %feed_back.1 = (f32[512,1024]{1,0:T(8,128)}, bf16[1024,512]{1,0:T(8,128)(2,1)S(1)}, f32[2,1024]{1,0:T(2,128)S(1)}) custom-call(f32[512,1024]{1,0:T(8,128)} %get-tuple-element.57.g3_ref, bf16[512,4096]{1,0:T(8,128)(2,1)} %get-tuple-element.58.slope_ref, bf16[512,512]{1,0:T(8,128)(2,1)S(1)} %copy-done.46, f32[512,1024]{1,0:T(8,128)} %get-tuple-element.60.n2_ref, ...), custom_call_target="tpu_custom_call" | custom-call | flops 10200547328 | bytes 16777216 | tf_op jit(solution)/shard_map/feed_back/pallas_call | solution.py:776
  196.9 3.1 collective-permute-start.21
  200.1 19.9 %cross_backward.1 = (bf16[1024,512]{1,0:T(8,128)(2,1)S(1)}, bf16[2,256,1024]{2,1,0:T(8,128)(2,1)S(1)}, bf16[2,256,1024]{2,1,0:T(8,128)(2,1)S(1)}, bf16[2,256,1024]{2,1,0:T(8,128)(2,1)}, bf16[2,256,1024]{2,1,0:T(8,128)(2,1)}) custom-call(bf16[512,1024]{1,0:T(8,128)(2,1)S(1)} %copy-done.44, bf16[16,1024,512]{2,1,0:T(8,128)(2,1)} %get-tuple-element.63.p_ref, ...), custom_call_target="tpu_custom_call" | custom-call | flops 17179869184 | bytes 16777216 | tf_op jit(solution)/shard_map/cross_backward/pallas_call | solution.py:291
  220.0 1.0 copy-done.27
  222.1 16.2 %first_back.1 = (f32[512,1024]{1,0:T(8,128)S(1)}, bf16[1024,512]{1,0:T(8,128)(2,1)S(1)}, f32[2,1024]{1,0:T(2,128)S(1)}) custom-call(f32[512,1024]{1,0:T(8,128)S(1)} %copy-done.22, bf16[1024,512]{1,0:T(8,128)(2,1)S(1)} %get-tuple-element.66.dqT_ref, f32[512,1024]{1,0:T(8,128)S(1)} %copy-done.21, f32[512,128]{1,0:T(8,128)S(1)} %get-tuple-element.67.r_ref, ...), custom_call_target="tpu_custom_call" | custom-call | flops 2147483648 | bytes 9437184 | tf_op jit(solution)/shard_map/first_back/pallas_call | solution.py:819
  238.2 1.3 copy-done.13
  240.5 1.4 collective-permute-start.22
  241.9 15.0 %self_backward.1 = (bf16[1024,512]{1,0:T(8,128)(2,1)S(1)}, bf16[2,256,1024]{2,1,0:T(8,128)(2,1)S(1)}, bf16[2,256,1024]{2,1,0:T(8,128)(2,1)S(1)}, bf16[2,256,1024]{2,1,0:T(8,128)(2,1)S(1)}, bf16[2,256,1024]{2,1,0:T(8,128)(2,1)}) custom-call(s32[7]{0:T(128)S(1)} %stack.93.sc_ref, bf16[256,1024]{1,0:T(8,128)(2,1)S(1)} %copy-done.36, ...), custom_call_target="tpu_custom_call" | custom-call | flops 10737418240 | bytes 10485760 | tf_op jit(solution)/shard_map/self_backward/pallas_call | solution.py:506
  256.9 1.0 copy-done.23
  257.8 1.0 copy-done.25
  258.8 1.0 copy-done.33
  261.1 3.0 maximum_select_fusion.4
  264.3 46.6 %all-gather.1 = f32[32,6,1024]{2,1,0:T(8,128)} all-gather(f32[1,6,1024]{2,1,0:T(8,128)S(1)} %maximum_bitcast_fusion), channel_id=2, replica_groups=mesh['dp'=8,'seq'=4] {'dp','seq'}, dimensions={0}, use_global_device_ids=true | all-gather | bytes 811008 | tf_op jit(solution)/shard_map/all_gather | solution.py:1021
  310.9 1.3 reduce_sum.9
  313.5 1.6 copy-done.2
  315.1 1.2 copy-done.30
  316.3 3.6 %enc_grad.2 = bf16[256,1024]{1,0:T(8,128)(2,1)S(1)} custom-call(bf16[2,256,1024]{2,1,0:T(8,128)(2,1)S(1)} %copy-done.30, bf16[2,256,1024]{2,1,0:T(8,128)(2,1)} %collective-permute-done.11.refs_1_, bf16[1024,1024]{1,0:T(8,128)(2,1)S(1)} %copy-done, bf16[1024,1024]{1,0:T(8,128)(2,1)S(1)} %copy-done.2), custom_call_target="tpu_custom_call" | custom-call | flops 1073741824 | bytes 4194304 | tf_op jit(solution)/shard_map/enc_grad/pallas_call | solution.py:851
  319.9 1.5 collective-permute-start.12
  321.4 1.6 copy-done.14
  323.0 1.2 copy-done.26
  324.2 4.5 %token_grad.2 = bf16[256,1024]{1,0:T(8,128)(2,1)S(1)} custom-call(f32[512,1024]{1,0:T(8,128)S(1)} %copy-done.14, bf16[1024,512]{1,0:T(8,128)(2,1)S(1)} %get-tuple-element.72.refs_1_, bf16[2,256,1024]{2,1,0:T(8,128)(2,1)S(1)} %copy-done.26, bf16[2,256,1024]{2,1,0:T(8,128)(2,1)} %collective-permute-done.8.refs_3_, bf16[1024,1024]{1,0:T(8,128)(2,1)S(1)} %copy-done.12, ...), custom_call_target="tpu_custom_call" | custom-call | flops 1610612736 | bytes 6291456 | tf_op jit(solution)/shard_map/token_grad/pallas_call | solution.py:886
  329.2 2.5 maximum_select_fusion.1
  331.8 3.6 %enc_grad.3 = bf16[256,1024]{1,0:T(8,128)(2,1)S(1)} custom-call(bf16[2,256,1024]{2,1,0:T(8,128)(2,1)S(1)} %copy-done.28, bf16[2,256,1024]{2,1,0:T(8,128)(2,1)} %collective-permute-done.13.refs_1_, bf16[1024,1024]{1,0:T(8,128)(2,1)S(1)} %copy-done, bf16[1024,1024]{1,0:T(8,128)(2,1)S(1)} %copy-done.3), custom_call_target="tpu_custom_call" | custom-call | flops 1073741824 | bytes 4194304 | tf_op jit(solution)/shard_map/enc_grad/pallas_call | solution.py:851
  335.4 4.4 %token_grad.3 = bf16[256,1024]{1,0:T(8,128)(2,1)S(1)} custom-call(f32[512,1024]{1,0:T(8,128)S(1)} %copy-done.15, bf16[1024,512]{1,0:T(8,128)(2,1)S(1)} %get-tuple-element.72.refs_1_, bf16[2,256,1024]{2,1,0:T(8,128)(2,1)S(1)} %copy-done.24, bf16[2,256,1024]{2,1,0:T(8,128)(2,1)} %collective-permute-done.10.refs_3_, bf16[1024,1024]{1,0:T(8,128)(2,1)S(1)} %copy-done.12, ...), custom_call_target="tpu_custom_call" | custom-call | flops 1610612736 | bytes 6291456 | tf_op jit(solution)/shard_map/token_grad/pallas_call | solution.py:886
  339.9 1.1 maximum_select_fusion.3
  341.0 4.0 %collective-permute-done.9 = bf16[256,1024]{1,0:T(8,128)(2,1)S(1)} collective-permute-done((bf16[256,1024]{1,0:T(8,128)(2,1)S(1)}, bf16[256,1024]{1,0:T(8,128)(2,1)S(1)}, u32[]{:S(2)}, u32[]{:S(2)}) %collective-permute-start.9) | collective-permute-done | bytes 524320 | tf_op jit(solution)/shard_map/ppermute | solution.py:949
  345.0 1.1 maximum_select_fusion.2
  346.1 3.3 maximum_select_fusion
  349.4 2.4 slice_convert_fusion
  351.9 2.9 copy.28
  (150 shorter events, 18.8 us)
Async XLA Ops:
  0.7 5.2 %copy-start = (bf16[1024,1024]{1,0:T(8,128)(2,1)S(1)}, bf16[1024,1024]{1,0:T(8,128)(2,1)}, u32[]{:S(2)}) copy-start(bf16[1024,1024]{1,0:T(8,128)(2,1)} %refs_2_.9) | copy-start | bytes 6291460
  0.7 5.2 %copy-start.1 = (bf16[1024,1024]{1,0:T(8,128)(2,1)S(1)}, bf16[1024,1024]{1,0:T(8,128)(2,1)}, u32[]{:S(2)}) copy-start(bf16[1024,1024]{1,0:T(8,128)(2,1)} %refs_3_.7) | copy-start | bytes 6291460
  2.1 14.8 %collective-permute-start = (bf16[256,1024]{1,0:T(8,128)(2,1)S(1)}, bf16[256,1024]{1,0:T(8,128)(2,1)S(1)}, u32[]{:S(2)}, u32[]{:S(2)}) collective-permute-start(bf16[256,1024]{1,0:T(8,128)(2,1)S(1)} %get-tuple-element.105), channel_id=1, source_target_pairs={{0,3},{1,2},{2,1},{3,0},{4,7},{5,6},{6,5},{7,4},{8,11},{9,10},{10,... | collective-permute-start | bytes 1572872 | tf_op jit(solution)/shard_map/ppermute | solution.py:946
  5.9 1.6 copy-start.4
  10.7 6.2 %copy-start.5 = (bf16[1024,1024]{1,0:T(8,128)(2,1)S(1)}, bf16[1024,1024]{1,0:T(8,128)(2,1)}, u32[]{:S(2)}) copy-start(bf16[1024,1024]{1,0:T(8,128)(2,1)} %refs_5_.5) | copy-start | bytes 6291460
  10.7 6.2 %copy-start.8 = (bf16[1024,1024]{1,0:T(8,128)(2,1)S(1)}, bf16[1024,1024]{1,0:T(8,128)(2,1)}, u32[]{:S(2)}) copy-start(bf16[1024,1024]{1,0:T(8,128)(2,1)} %refs_6_.5) | copy-start | bytes 6291460
  10.7 6.2 %copy-start.11 = (bf16[1024,1024]{1,0:T(8,128)(2,1)S(1)}, bf16[1024,1024]{1,0:T(8,128)(2,1)}, u32[]{:S(2)}) copy-start(bf16[1024,1024]{1,0:T(8,128)(2,1)} %refs_4_.5) | copy-start | bytes 6291460
  15.9 3.8 %copy-start.34 = (bf16[256,1024]{1,0:T(8,128)(2,1)}, bf16[256,1024]{1,0:T(8,128)(2,1)S(1)}, u32[]{:S(2)}) copy-start(bf16[256,1024]{1,0:T(8,128)(2,1)S(1)} %get-tuple-element.46.q_own) | copy-start | bytes 1572868
  15.9 27.6 %collective-permute-start.1 = (bf16[2,256,1024]{2,1,0:T(8,128)(2,1)}, bf16[2,256,1024]{2,1,0:T(8,128)(2,1)}, u32[]{:S(2)}, u32[]{:S(2)}) collective-permute-start(bf16[2,256,1024]{2,1,0:T(8,128)(2,1)} %get-tuple-element.48.refs_0_), channel_id=1, source_target_pairs={{1,0},{0,1},{2,3},{3,2},{5,4},{4,5},{6,7},{7,6},{9,8},{8,9},{10,11... | collective-permute-start | bytes 3145736 | tf_op jit(solution)/shard_map/ppermute | solution.py:984
  19.8 17.6 %copy-start.37 = (bf16[256,1024]{1,0:T(8,128)(2,1)}, bf16[256,1024]{1,0:T(8,128)(2,1)S(1)}, u32[]{:S(2)}) copy-start(bf16[256,1024]{1,0:T(8,128)(2,1)S(1)} %get-tuple-element.47.q_swap) | copy-start | bytes 1572868
  19.8 23.8 %collective-permute-start.2 = (bf16[2,256,1024]{2,1,0:T(8,128)(2,1)}, bf16[2,256,1024]{2,1,0:T(8,128)(2,1)}, u32[]{:S(2)}, u32[]{:S(2)}) collective-permute-start(bf16[2,256,1024]{2,1,0:T(8,128)(2,1)} %get-tuple-element.49.refs_1_), channel_id=1, source_target_pairs={{1,0},{0,1},{2,3},{3,2},{5,4},{4,5},{6,7},{7,6},{9,8},{8,9},{10,11... | collective-permute-start | bytes 3145736 | tf_op jit(solution)/shard_map/ppermute | solution.py:984
  19.9 14.7 %collective-permute-start.3 = (bf16[256,1024]{1,0:T(8,128)(2,1)S(1)}, bf16[256,1024]{1,0:T(8,128)(2,1)S(1)}, u32[]{:S(2)}, u32[]{:S(2)}) collective-permute-start(bf16[256,1024]{1,0:T(8,128)(2,1)S(1)} %get-tuple-element.103), channel_id=1, source_target_pairs={{0,3},{1,2},{2,1},{3,0},{4,7},{5,6},{6,5},{7,4},{8,11},{9,10},{10,... | collective-permute-start | bytes 1572872 | tf_op jit(solution)/shard_map/ppermute | solution.py:946
  22.4 15.1 %copy-start.52 = (bf16[2,256,1024]{2,1,0:T(8,128)(2,1)S(1)}, bf16[2,256,1024]{2,1,0:T(8,128)(2,1)}, u32[]{:S(2)}) copy-start(bf16[2,256,1024]{2,1,0:T(8,128)(2,1)} %param.25) | copy-start | bytes 3145732
  22.4 46.3 %collective-permute-start.4 = (bf16[2,256,1024]{2,1,0:T(8,128)(2,1)}, bf16[2,256,1024]{2,1,0:T(8,128)(2,1)}, u32[]{:S(2)}, u32[]{:S(2)}) collective-permute-start(bf16[2,256,1024]{2,1,0:T(8,128)(2,1)} %get-tuple-element.52.refs_0_), channel_id=1, source_target_pairs={{1,0},{0,1},{2,3},{3,2},{5,4},{4,5},{6,7},{7,6},{9,8},{8,9},{10,11... | collective-permute-start | bytes 3145736 | tf_op jit(solution)/shard_map/ppermute | solution.py:984
  37.3 2.8 copy-start.56
  37.3 3.5 copy-start.57
  37.3 4.1 %copy-start.58 = (s32[2]{0:T(128)S(1)}, s32[2]{0:T(128)}, u32[]{:S(2)}) copy-start(s32[2]{0:T(128)} %param.24) | copy-start | bytes 28
  37.4 31.4 %collective-permute-start.5 = (bf16[2,256,1024]{2,1,0:T(8,128)(2,1)}, bf16[2,256,1024]{2,1,0:T(8,128)(2,1)}, u32[]{:S(2)}, u32[]{:S(2)}) collective-permute-start(bf16[2,256,1024]{2,1,0:T(8,128)(2,1)} %project_enc.1.refs_1_), channel_id=1, source_target_pairs={{1,0},{0,1},{2,3},{3,2},{5,4},{4,5},{6,7},{7,6},{9,8},{8,9},{10,11... | collective-permute-start | bytes 3145736 | tf_op jit(solution)/shard_map/ppermute | solution.py:984
  38.6 49.9 %collective-permute-start.6 = (bf16[256,1024]{1,0:T(8,128)(2,1)}, bf16[256,1024]{1,0:T(8,128)(2,1)}, u32[]{:S(2)}, u32[]{:S(2)}) collective-permute-start(bf16[256,1024]{1,0:T(8,128)(2,1)} %get-tuple-element.101), channel_id=1, source_target_pairs={{0,3},{1,2},{2,1},{3,0},{4,7},{5,6},{6,5},{7,4},{8,11},{9,10},{10,... | collective-permute-start | bytes 1572872 | tf_op jit(solution)/shard_map/ppermute | solution.py:946
  45.6 17.1 %copy-start.16 = (bf16[1024,1024]{1,0:T(8,128)(2,1)S(1)}, bf16[1024,1024]{1,0:T(8,128)(2,1)}, u32[]{:S(2)}) copy-start(bf16[1024,1024]{1,0:T(8,128)(2,1)} %w_out.7) | copy-start | bytes 6291460
  45.6 17.1 %copy-start.18 = (bf16[1024,1024]{1,0:T(8,128)(2,1)S(1)}, bf16[1024,1024]{1,0:T(8,128)(2,1)}, u32[]{:S(2)}) copy-start(bf16[1024,1024]{1,0:T(8,128)(2,1)} %w_query.3) | copy-start | bytes 6291460
  45.6 17.1 %copy-start.31 = (f32[3,1024]{1,0:T(4,128)S(1)}, f32[3,1024]{1,0:T(4,128)}, u32[]{:S(2)}) copy-start(f32[3,1024]{1,0:T(4,128)} %gain_ref.7) | copy-start | bytes 36868
  45.6 17.1 %copy-start.40 = (f32[3,1024]{1,0:T(4,128)S(1)}, f32[3,1024]{1,0:T(4,128)}, u32[]{:S(2)}) copy-start(f32[3,1024]{1,0:T(4,128)} %bias_ref.3) | copy-start | bytes 36868
  58.8 4.0 %copy-start.45 = (bf16[16,5,256,256]{3,2,1,0:T(8,128)(2,1)}, bf16[16,5,256,256]{3,2,1,0:T(8,128)(2,1)S(1)}, u32[]{:S(2)}) copy-start(bf16[16,5,256,256]{3,2,1,0:T(8,128)(2,1)S(1)} %get-tuple-element.69.p_ref) | copy-start | bytes 31457284
  62.8 4.7 %copy-start.41 = (bf16[1024,512]{1,0:T(8,128)(2,1)}, bf16[1024,512]{1,0:T(8,128)(2,1)S(1)}, u32[]{:S(2)}) copy-start(bf16[1024,512]{1,0:T(8,128)(2,1)S(1)} %get-tuple-element.50.oT_ref) | copy-start | bytes 3145732
  68.8 18.7 %copy-start.43 = (bf16[512,1024]{1,0:T(8,128)(2,1)}, bf16[512,1024]{1,0:T(8,128)(2,1)S(1)}, u32[]{:S(2)}) copy-start(bf16[512,1024]{1,0:T(8,128)(2,1)S(1)} %get-tuple-element.51.q_ref) | copy-start | bytes 3145732
  123.0 2.9 collective-permute-start.14
  129.6 14.4 %collective-permute-start.15 = (bf16[256,1024]{1,0:T(8,128)(2,1)}, bf16[256,1024]{1,0:T(8,128)(2,1)}, u32[]{:S(2)}, u32[]{:S(2)}) collective-permute-start(bf16[256,1024]{1,0:T(8,128)(2,1)} %constant_dynamic-slice_fusion.3), channel_id=1, source_target_pairs={{0,4},{4,0},{8,12},{12,8},{16,20},{20,16},{24,28},{28,24},{1,5},{5... | collective-permute-start | bytes 1572872 | tf_op jit(solution)/shard_map/ppermute | solution.py:899
  131.0 45.1 %copy-start.32 = (f32[3,1024]{1,0:T(4,128)S(1)}, f32[3,1024]{1,0:T(4,128)}, u32[]{:S(2)}) copy-start(f32[3,1024]{1,0:T(4,128)} %gain_ref.7) | copy-start | bytes 36868
  131.0 45.1 %copy-start.46 = (bf16[512,512]{1,0:T(8,128)(2,1)S(1)}, bf16[512,512]{1,0:T(8,128)(2,1)}, u32[]{:S(2)}) copy-start(bf16[512,512]{1,0:T(8,128)(2,1)} %get-tuple-element.59.gai_ref) | copy-start | bytes 1572868
  131.0 45.1 %copy-start.47 = (f32[512,128]{1,0:T(8,128)S(1)}, f32[512,128]{1,0:T(8,128)}, u32[]{:S(2)}) copy-start(f32[512,128]{1,0:T(8,128)} %get-tuple-element.61.r2_ref) | copy-start | bytes 786436
  146.3 7.9 %collective-permute-start.16 = (bf16[128,1024]{1,0:T(8,128)(2,1)S(1)}, bf16[128,1024]{1,0:T(8,128)(2,1)}, u32[]{:S(2)}, u32[]{:S(2)}) collective-permute-start(bf16[128,1024]{1,0:T(8,128)(2,1)S(1)} %constant_dynamic-slice_fusion.2), channel_id=1, source_target_pairs={{0,8},{4,12},{8,0},{12,4},{16,24},{20,28},{24,16},{28,20},{1,9},{5... | collective-permute-start | bytes 786440 | tf_op jit(solution)/shard_map/ppermute | solution.py:899
  155.9 8.1 %collective-permute-start.17 = (bf16[64,1024]{1,0:T(8,128)(2,1)}, bf16[64,1024]{1,0:T(8,128)(2,1)}, u32[]{:S(2)}, u32[]{:S(2)}) collective-permute-start(bf16[64,1024]{1,0:T(8,128)(2,1)} %constant_dynamic-slice_fusion.1), channel_id=1, source_target_pairs={{0,16},{4,20},{8,24},{12,28},{16,0},{20,4},{24,8},{28,12},{1,17},{... | collective-permute-start | bytes 393224 | tf_op jit(solution)/shard_map/ppermute | solution.py:899
  165.6 4.5 %collective-permute-start.18 = (bf16[32,1024]{1,0:T(8,128)(2,1)S(1)}, bf16[32,1024]{1,0:T(8,128)(2,1)S(1)}, u32[]{:S(2)}, u32[]{:S(2)}) collective-permute-start(bf16[32,1024]{1,0:T(8,128)(2,1)S(1)} %constant_dynamic-slice_fusion), channel_id=1, source_target_pairs={{0,2},{1,3},{2,0},{3,1},{4,6},{5,7},{6,4},{7,5},{8,10},{9,11},{10,... | collective-permute-start | bytes 196616 | tf_op jit(solution)/shard_map/ppermute | solution.py:899
  170.9 4.3 %collective-permute-start.19 = (bf16[32,1024]{1,0:T(8,128)(2,1)S(1)}, bf16[32,1024]{1,0:T(8,128)(2,1)S(1)}, u32[]{:S(2)}, u32[]{:S(2)}) collective-permute-start(bf16[32,1024]{1,0:T(8,128)(2,1)S(1)} %add_convert_fusion.4), channel_id=1, source_target_pairs={{0,2},{1,3},{2,0},{3,1},{4,6},{5,7},{6,4},{7,5},{8,10},{9,11},{10,... | collective-permute-start | bytes 196616 | tf_op jit(solution)/shard_map/ppermute | solution.py:899
  175.3 21.6 %collective-permute-start.20 = (bf16[64,1024]{1,0:T(8,128)(2,1)S(1)}, bf16[64,1024]{1,0:T(8,128)(2,1)S(1)}, u32[]{:S(2)}, u32[]{:S(2)}) collective-permute-start(bf16[64,1024]{1,0:T(8,128)(2,1)S(1)} %maximum_select_fusion.7), channel_id=1, source_target_pairs={{0,16},{4,20},{8,24},{12,28},{16,0},{20,4},{24,8},{28,12},{1,17},{... | collective-permute-start | bytes 393224 | tf_op jit(solution)/shard_map/ppermute | solution.py:899
  176.2 23.9 %copy-start.44 = (bf16[512,1024]{1,0:T(8,128)(2,1)S(1)}, bf16[512,1024]{1,0:T(8,128)(2,1)}, u32[]{:S(2)}) copy-start(bf16[512,1024]{1,0:T(8,128)(2,1)} %copy-done.43) | copy-start | bytes 3145732
  176.2 23.9 %copy-start.49 = (bf16[1024,512]{1,0:T(8,128)(2,1)S(1)}, bf16[1024,512]{1,0:T(8,128)(2,1)}, u32[]{:S(2)}) copy-start(bf16[1024,512]{1,0:T(8,128)(2,1)} %copy-done.48) | copy-start | bytes 3145732
  196.9 42.6 %collective-permute-start.21 = (bf16[128,1024]{1,0:T(8,128)(2,1)S(1)}, bf16[128,1024]{1,0:T(8,128)(2,1)S(1)}, u32[]{:S(2)}, u32[]{:S(2)}) collective-permute-start(bf16[128,1024]{1,0:T(8,128)(2,1)S(1)} %maximum_select_fusion.6), channel_id=1, source_target_pairs={{0,8},{4,12},{8,0},{12,4},{16,24},{20,28},{24,16},{28,20},{1,9},{5... | collective-permute-start | bytes 786440 | tf_op jit(solution)/shard_map/ppermute | solution.py:899
  200.1 21.9 %copy-start.17 = (bf16[1024,1024]{1,0:T(8,128)(2,1)S(1)}, bf16[1024,1024]{1,0:T(8,128)(2,1)}, u32[]{:S(2)}) copy-start(bf16[1024,1024]{1,0:T(8,128)(2,1)} %w_out.7) | copy-start | bytes 6291460
  200.1 21.9 %copy-start.19 = (bf16[1024,1024]{1,0:T(8,128)(2,1)S(1)}, bf16[1024,1024]{1,0:T(8,128)(2,1)}, u32[]{:S(2)}) copy-start(bf16[1024,1024]{1,0:T(8,128)(2,1)} %w_query.3) | copy-start | bytes 6291460
  200.1 21.9 %copy-start.21 = (f32[512,1024]{1,0:T(8,128)S(1)}, f32[512,1024]{1,0:T(8,128)}, u32[]{:S(2)}) copy-start(f32[512,1024]{1,0:T(8,128)} %copy-done.20) | copy-start | bytes 6291460
  200.1 21.9 %copy-start.22 = (f32[512,1024]{1,0:T(8,128)S(1)}, f32[512,1024]{1,0:T(8,128)}, u32[]{:S(2)}) copy-start(f32[512,1024]{1,0:T(8,128)} %get-tuple-element.62.g2_ref) | copy-start | bytes 6291460
  222.0 42.1 %collective-permute-start.11 = (bf16[2,256,1024]{2,1,0:T(8,128)(2,1)}, bf16[2,256,1024]{2,1,0:T(8,128)(2,1)}, u32[]{:S(2)}, u32[]{:S(2)}) collective-permute-start(bf16[2,256,1024]{2,1,0:T(8,128)(2,1)} %get-tuple-element.78), channel_id=1, source_target_pairs={{0,1},{1,0},{3,2},{2,3},{4,5},{5,4},{7,6},{6,7},{8,9},{9,8},{11,10... | collective-permute-start | bytes 3145736 | tf_op jit(solution)/shard_map/ppermute | solution.py:1011
  222.0 19.9 %copy-start.36 = (bf16[256,1024]{1,0:T(8,128)(2,1)S(1)}, bf16[256,1024]{1,0:T(8,128)(2,1)}, u32[]{:S(2)}) copy-start(bf16[256,1024]{1,0:T(8,128)(2,1)} %copy-done.34) | copy-start | bytes 1572868
  222.0 19.9 %copy-start.39 = (bf16[256,1024]{1,0:T(8,128)(2,1)S(1)}, bf16[256,1024]{1,0:T(8,128)(2,1)}, u32[]{:S(2)}) copy-start(bf16[256,1024]{1,0:T(8,128)(2,1)} %copy-done.37) | copy-start | bytes 1572868
  222.0 19.8 %copy-start.42 = (bf16[1024,512]{1,0:T(8,128)(2,1)S(1)}, bf16[1024,512]{1,0:T(8,128)(2,1)}, u32[]{:S(2)}) copy-start(bf16[1024,512]{1,0:T(8,128)(2,1)} %copy-done.41) | copy-start | bytes 3145732
  240.5 20.1 %collective-permute-start.22 = (bf16[256,1024]{1,0:T(8,128)(2,1)}, bf16[256,1024]{1,0:T(8,128)(2,1)}, u32[]{:S(2)}, u32[]{:S(2)}) collective-permute-start(bf16[256,1024]{1,0:T(8,128)(2,1)} %maximum_select_fusion.5), channel_id=1, source_target_pairs={{0,4},{4,0},{8,12},{12,8},{16,20},{20,16},{24,28},{28,24},{1,5},{5... | collective-permute-start | bytes 1572872 | tf_op jit(solution)/shard_map/ppermute | solution.py:899
  241.9 18.7 %copy-start.55 = (f32[2,1024]{1,0:T(2,128)S(1)}, f32[2,1024]{1,0:T(2,128)}, u32[]{:S(2)}) copy-start(f32[2,1024]{1,0:T(2,128)} %get-tuple-element.84) | copy-start | bytes 24580
  259.8 60.1 %collective-permute-start.8 = (bf16[2,256,1024]{2,1,0:T(8,128)(2,1)}, bf16[2,256,1024]{2,1,0:T(8,128)(2,1)}, u32[]{:S(2)}, u32[]{:S(2)}) collective-permute-start(bf16[2,256,1024]{2,1,0:T(8,128)(2,1)} %get-tuple-element.74), channel_id=1, source_target_pairs={{0,1},{1,0},{3,2},{2,3},{4,5},{5,4},{7,6},{6,7},{8,9},{9,8},{11,10... | collective-permute-start | bytes 3145736 | tf_op jit(solution)/shard_map/ppermute | solution.py:1011
  260.0 71.7 %collective-permute-start.13 = (bf16[2,256,1024]{2,1,0:T(8,128)(2,1)}, bf16[2,256,1024]{2,1,0:T(8,128)(2,1)}, u32[]{:S(2)}, u32[]{:S(2)}) collective-permute-start(bf16[2,256,1024]{2,1,0:T(8,128)(2,1)} %get-tuple-element.80), channel_id=1, source_target_pairs={{0,1},{1,0},{3,2},{2,3},{4,5},{5,4},{7,6},{6,7},{8,9},{9,8},{11,10... | collective-permute-start | bytes 3145736 | tf_op jit(solution)/shard_map/ppermute | solution.py:1010
  260.3 75.0 %collective-permute-start.10 = (bf16[2,256,1024]{2,1,0:T(8,128)(2,1)}, bf16[2,256,1024]{2,1,0:T(8,128)(2,1)}, u32[]{:S(2)}, u32[]{:S(2)}) collective-permute-start(bf16[2,256,1024]{2,1,0:T(8,128)(2,1)} %copy-done.33), channel_id=1, source_target_pairs={{0,1},{1,0},{3,2},{2,3},{4,5},{5,4},{7,6},{6,7},{8,9},{9,8},{11,10... | collective-permute-start | bytes 3145736 | tf_op jit(solution)/shard_map/ppermute | solution.py:1010
  260.6 68.2 %collective-permute-start.7 = (bf16[256,1024]{1,0:T(8,128)(2,1)}, bf16[256,1024]{1,0:T(8,128)(2,1)}, u32[]{:S(2)}, u32[]{:S(2)}) collective-permute-start(bf16[256,1024]{1,0:T(8,128)(2,1)} %get-tuple-element.55), channel_id=1, source_target_pairs={{0,3},{1,2},{2,1},{3,0},{4,7},{5,6},{6,5},{7,4},{8,11},{9,10},{10,... | collective-permute-start | bytes 1572872 | tf_op jit(solution)/shard_map/ppermute | solution.py:949
  264.1 82.0 %collective-permute-start.23 = (bf16[512,1024]{1,0:T(8,128)(2,1)}, bf16[512,1024]{1,0:T(8,128)(2,1)}, u32[]{:S(2)}, u32[]{:S(2)}) collective-permute-start(bf16[512,1024]{1,0:T(8,128)(2,1)} %maximum_select_fusion.4), channel_id=1, source_target_pairs={{0,1},{1,0},{2,3},{3,2},{4,5},{5,4},{6,7},{7,6},{8,9},{9,8},{10,11... | collective-permute-start | bytes 3145736 | tf_op jit(solution)/shard_map/ppermute | solution.py:899
  316.3 5.1 %copy-start.6 = (bf16[1024,1024]{1,0:T(8,128)(2,1)S(1)}, bf16[1024,1024]{1,0:T(8,128)(2,1)}, u32[]{:S(2)}) copy-start(bf16[1024,1024]{1,0:T(8,128)(2,1)} %refs_5_.5) | copy-start | bytes 6291460
  316.3 5.1 %copy-start.9 = (bf16[1024,1024]{1,0:T(8,128)(2,1)S(1)}, bf16[1024,1024]{1,0:T(8,128)(2,1)}, u32[]{:S(2)}) copy-start(bf16[1024,1024]{1,0:T(8,128)(2,1)} %refs_6_.5) | copy-start | bytes 6291460
  316.3 5.1 %copy-start.12 = (bf16[1024,1024]{1,0:T(8,128)(2,1)S(1)}, bf16[1024,1024]{1,0:T(8,128)(2,1)}, u32[]{:S(2)}) copy-start(bf16[1024,1024]{1,0:T(8,128)(2,1)} %refs_4_.5) | copy-start | bytes 6291460
  319.9 19.9 %collective-permute-start.12 = (bf16[256,1024]{1,0:T(8,128)(2,1)S(1)}, bf16[256,1024]{1,0:T(8,128)(2,1)S(1)}, u32[]{:S(2)}, u32[]{:S(2)}) collective-permute-start(bf16[256,1024]{1,0:T(8,128)(2,1)S(1)} %enc_grad.2), channel_id=1, source_target_pairs={{0,3},{1,2},{2,1},{3,0},{4,7},{5,6},{6,5},{7,4},{8,11},{9,10},{10,... | collective-permute-start | bytes 1572872 | tf_op jit(solution)/shard_map/ppermute | solution.py:949
  324.2 5.0 %copy-start.53 = (bf16[256,1024]{1,0:T(8,128)(2,1)S(1)}, bf16[256,1024]{1,0:T(8,128)(2,1)}, u32[]{:S(2)}) copy-start(bf16[256,1024]{1,0:T(8,128)(2,1)} %get-tuple-element.56) | copy-start | bytes 1572868
  324.2 7.5 %copy-start.28 = (bf16[2,256,1024]{2,1,0:T(8,128)(2,1)S(1)}, bf16[2,256,1024]{2,1,0:T(8,128)(2,1)}, u32[]{:S(2)}) copy-start(bf16[2,256,1024]{2,1,0:T(8,128)(2,1)} %copy-done.27) | copy-start | bytes 3145732
  328.8 3.0 copy-start.3
  328.8 16.2 %collective-permute-start.9 = (bf16[256,1024]{1,0:T(8,128)(2,1)S(1)}, bf16[256,1024]{1,0:T(8,128)(2,1)S(1)}, u32[]{:S(2)}, u32[]{:S(2)}) collective-permute-start(bf16[256,1024]{1,0:T(8,128)(2,1)S(1)} %token_grad.2), channel_id=1, source_target_pairs={{0,3},{1,2},{2,1},{3,0},{4,7},{5,6},{6,5},{7,4},{8,11},{9,10},{10,... | collective-permute-start | bytes 1572872 | tf_op jit(solution)/shard_map/ppermute | solution.py:949
  331.7 3.6 %copy-start.15 = (f32[512,1024]{1,0:T(8,128)S(1)}, f32[512,1024]{1,0:T(8,128)}, u32[]{:S(2)}) copy-start(f32[512,1024]{1,0:T(8,128)} %copy-done.13) | copy-start | bytes 6291460
  331.8 3.6 %copy-start.24 = (bf16[2,256,1024]{2,1,0:T(8,128)(2,1)S(1)}, bf16[2,256,1024]{2,1,0:T(8,128)(2,1)}, u32[]{:S(2)}) copy-start(bf16[2,256,1024]{2,1,0:T(8,128)(2,1)} %copy-done.23) | copy-start | bytes 3145732
  (19 other events, 21.8 us)
